TPU v7x, 32 devices: a whole 2x2x4 slice. The times are simulated.
32 devices in a mesh: member: 2 (over y), lat: 8 (over z, core), lon: 2 (over x), lev: 1.
Axes of the slice: x: 2, y: 2, z: 4, core: 2. Of those that a mesh axis runs over, the one named last changes fastest.
Arguments:
- adjoint: float32 [6, 32, 64, 3072], P('member', 'lev', 'lat', 'lon'), parts along dimension 0, may hold values from -6 to 6
- depth: bfloat16 [32, 64, 3072], P('lev', 'lat', 'lon'), may hold values from 0.5 to 2
- zonal_coef: float32 [64], replicated, may hold values from 0.05 to 0.5
- merid_coef: float32 [64], replicated, may hold values from 0.05 to 0.5
- coriolis: float32 [64], replicated, may hold values from -0.5 to 0.5
- layer_weight: float32 [32], P('lev'), may hold values from 0.02 to 0.2
- cutoffs: int32 [64], replicated, may hold values from 0 to 1023, as said below
- polar_flags: int32 [64], replicated, may hold values from 0 to 1, as said below
Outputs:
- adjoint_next: float32 [6, 32, 64, 3072], P('member', 'lev', 'lat', 'lon'), parts along dimension 0
There are 2 independent parts, one for each index of `member`. A program takes and returns all parts, laid end to end along the dimension named above; an argument that names none is the same for every part. Nothing has to cross between parts.
Inputs may be any that keep to these rules, and one draw needn't show every extreme that they name: cutoffs[0] is 1023 and cutoffs[63] is 0. `polar_flags`: the flagged rows form one run that starts at row 0 and one that ends at row 63; each run has 12 to 24 rows, and one of the two has exactly 24.
All inputs are finite; a program needn't handle non-finite values.
Results may differ from a plain program's by a relative error of at most 0.0003.
Values sent between devices are 32-bit elements; how exact they have to be, the bound alone decides.
A program may use at most 128 MiB of HBM per device.

v0:
```python
import math

import jax
import jax.numpy as jnp
from jax import lax
from jax.sharding import PartitionSpec as P

KMAX = 1024
POLE_ROWS = 24


def extended(cells, sides, width, closed):
    for axis, dim in sides:
        count = lax.axis_size(axis)
        ends = count if closed else count - 1
        head = lax.slice_in_dim(cells, 0, width, axis=dim)
        tail = lax.slice_in_dim(cells, cells.shape[dim] - width, cells.shape[dim], axis=dim)
        cells = jnp.concatenate(
            [
                lax.ppermute(tail, axis, [(i, (i + 1) % count) for i in range(ends)]),
                cells,
                lax.ppermute(head, axis, [((i + 1) % count, i) for i in range(ends)]),
            ],
            axis=dim,
        )
    return cells


def entering(value, axis, join, neutral):
    count, mine = (lax.axis_size(axis), lax.axis_index(axis))
    pieces = lax.all_gather(value, axis)
    total = jnp.full_like(value, 0) + jnp.asarray(neutral, value.dtype)

    def turn(position, total):
        longer = join(total, pieces[position])
        return jnp.where(position < mine, longer, total)

    return lax.fori_loop(0, count - 1, turn, total)


def wave_table(col_count, wave_start, wave_count, circle):
    columns = lax.iota(jnp.int32, col_count)
    wave_index = wave_start + lax.iota(jnp.int32, wave_count)
    phase = columns[:, None] * wave_index[None, :] % circle
    angle = phase.astype(jnp.float32) * (2.0 * math.pi / circle)
    return jnp.concatenate([jnp.cos(angle), jnp.sin(angle)], axis=1)


def keep_weights(cut_rows, wave_start, wave_count, circle):
    wave_index = wave_start + lax.iota(jnp.int32, wave_count)
    factor = jnp.where(wave_index == 0, 1.0, 2.0) / circle
    kept = (wave_index[None, :] <= cut_rows[:, None]).astype(jnp.float32) * factor[None, :]
    return jnp.concatenate([kept, kept], axis=1)


def block_width():
    return min(KMAX, 128)


def project_rows(row_data, cut_rows):
    circle = row_data.shape[1]
    width = block_width()
    result = jnp.zeros(row_data.shape, jnp.float32)
    for block_index in range(KMAX // width):
        table = wave_table(circle, block_index * width, width, circle)
        coefs = jnp.dot(
            row_data, table, precision=lax.Precision.HIGHEST, preferred_element_type=jnp.float32
        )
        weights = keep_weights(cut_rows, block_index * width, width, circle)
        result = result + jnp.dot(
            coefs * weights,
            table.T,
            precision=lax.Precision.HIGHEST,
            preferred_element_type=jnp.float32,
        )
    return result


def transpose_filter(row_data, cut_rows, flag_rows):
    lon_count = lax.axis_size("lon")
    lon_index = lax.axis_index("lon")
    share = row_data.shape[0] // lon_count
    full_rows = lax.all_to_all(row_data, "lon", split_axis=0, concat_axis=1, tiled=True)
    my_cuts = lax.dynamic_slice_in_dim(cut_rows, lon_index * share, share)
    smoothed = project_rows(full_rows, my_cuts)
    returned = lax.all_to_all(smoothed, "lon", split_axis=1, concat_axis=0, tiled=True)
    return jnp.where(flag_rows[:, None] > 0, returned, row_data)


def polar_filter(row_data, cut_rows, flag_rows):
    return transpose_filter(row_data, cut_rows, flag_rows)


def on_device(adjoint, depth, zonal_coef, merid_coef, coriolis, layer_weight, cutoffs, polar_flags):
    fields, level_count, lat_rows, lon_cells = adjoint.shape
    lat_index = lax.axis_index("lat")
    lat_total = lat_rows * lax.axis_size("lat")
    stacked = adjoint.reshape(fields * level_count, lat_rows, lon_cells)
    bands = lax.all_to_all(stacked, "lat", split_axis=0, concat_axis=1, tiled=True)
    groups = bands.shape[0]
    polar_block = jnp.concatenate([bands[:, :POLE_ROWS], bands[:, lat_total - POLE_ROWS :]], axis=1)
    polar_cuts = jnp.concatenate([cutoffs[:POLE_ROWS], cutoffs[lat_total - POLE_ROWS :]])
    polar_marks = jnp.concatenate([polar_flags[:POLE_ROWS], polar_flags[lat_total - POLE_ROWS :]])
    row_data = polar_block.reshape(groups * 2 * POLE_ROWS, lon_cells)
    cut_rows = jnp.tile(polar_cuts, groups)
    flag_rows = jnp.tile(polar_marks, groups)
    treated = polar_filter(row_data, cut_rows, flag_rows)
    treated = treated.reshape(groups, 2 * POLE_ROWS, lon_cells)
    bands = jnp.concatenate(
        [
            treated[:, :POLE_ROWS],
            bands[:, POLE_ROWS : lat_total - POLE_ROWS],
            treated[:, POLE_ROWS:],
        ],
        axis=1,
    )
    filtered = lax.all_to_all(bands, "lat", split_axis=1, concat_axis=0, tiled=True).reshape(
        adjoint.shape
    )
    q_height = filtered[0]
    q_east = filtered[1]
    q_north = filtered[2]
    zonal_rows = lax.dynamic_slice_in_dim(zonal_coef, lat_index * lat_rows, lat_rows)[None, :, None]
    merid_rows = lax.dynamic_slice_in_dim(merid_coef, lat_index * lat_rows, lat_rows)[None, :, None]
    coriolis_rows = lax.dynamic_slice_in_dim(coriolis, lat_index * lat_rows, lat_rows)[
        None, :, None
    ]
    height_flux = depth.astype(jnp.float32) * q_height
    north_pair = jnp.stack([merid_rows * q_north, merid_rows * height_flux])
    north_rims = extended(north_pair, (("lat", 2),), 1, False)
    merid_diff = north_rims[:, :, :-2] - north_rims[:, :, 2:]
    east_pair = jnp.stack([q_east, height_flux])
    east_rims = extended(east_pair, (("lon", 3),), 1, True)
    zonal_diff = zonal_rows * (east_rims[..., :-2] - east_rims[..., 2:])
    column_force = -zonal_diff[0] - merid_diff[0]
    running = jnp.cumsum(column_force, axis=0)
    carried = entering(
        jnp.sum(column_force, axis=0), "lev", jnp.add, jnp.zeros((lat_rows, lon_cells), jnp.float32)
    )
    new_height = adjoint[0] + layer_weight[:, None, None] * (running + carried[None])
    new_east = adjoint[1] - zonal_diff[1] - coriolis_rows * q_north
    new_north = adjoint[2] - merid_diff[1] + coriolis_rows * q_east
    return jnp.stack([new_height, new_east, new_north])


def solution(mesh):
    return jax.shard_map(
        on_device,
        mesh=mesh,
        in_specs=(
            P("member", "lev", "lat", "lon"),
            P("lev", "lat", "lon"),
            P(),
            P(),
            P(),
            P("lev"),
            P(),
            P(),
        ),
        out_specs=P("member", "lev", "lat", "lon"),
        check_vma=False,
    )
```

profile of v0, /device:TPU:1, one launch (start us, length us, event | category | flops | bytes accessed | tf_op | source)
XLA Modules:
  0.0 448.5 jit_solution(4146871428329461168)
XLA Ops:
  0.0 6.5 %all-to-all-start = ((f32[96,8,1536]{2,1,0:T(8,128)}), f32[96,8,1536]{2,1,0:T(8,128)}, u32[]{:S(2)}, u32[]{:S(2)}) async-start(f32[96,8,1536]{2,1,0:T(8,128)} %bitcast.64), calls=%async_computation | async-start | bytes 9437184 | tf_op jit(solution)/shard_map/all_to_all | solution.py:99
  9.4 8.2 %fusion.62 = (f32[3072,128]{1,0:T(8,128)}, f32[3072,128]{1,0:T(8,128)}) fusion(), kind=kLoop, calls=%fused_computation.114 | loop fusion | flops 3538944 | bytes 3145728 | tf_op jit(solution)/shard_map/sin | solution.py:46
  17.5 7.3 %fusion.59 = (f32[3072,128]{1,0:T(8,128)}, f32[3072,128]{1,0:T(8,128)}) fusion(s32[128]{0:T(128)S(1)} %iota_add_fusion.6), kind=kLoop, calls=%fused_computation.110 | loop fusion | flops 3538944 | bytes 3146240 | tf_op jit(solution)/shard_map/cos | solution.py:46
  24.9 7.3 %fusion.55 = (f32[3072,128]{1,0:T(8,128)}, f32[3072,128]{1,0:T(8,128)}) fusion(s32[128]{0:T(128)S(1)} %get-tuple-element.59), kind=kLoop, calls=%fused_computation.105 | loop fusion | flops 3538944 | bytes 3146240 | tf_op jit(solution)/shard_map/cos | solution.py:46
  32.2 7.3 %fusion.51 = (f32[3072,128]{1,0:T(8,128)}, f32[3072,128]{1,0:T(8,128)}) fusion(s32[128]{0:T(128)S(1)} %get-tuple-element.58), kind=kLoop, calls=%fused_computation.100 | loop fusion | flops 3538944 | bytes 3146240 | tf_op jit(solution)/shard_map/cos | solution.py:46
  39.5 7.3 %fusion.47 = (f32[3072,128]{1,0:T(8,128)}, f32[3072,128]{1,0:T(8,128)}) fusion(s32[128]{0:T(128)S(1)} %get-tuple-element.57), kind=kLoop, calls=%fused_computation.95 | loop fusion | flops 3538944 | bytes 3146240 | tf_op jit(solution)/shard_map/cos | solution.py:46
  46.9 7.3 %fusion.43 = (f32[3072,128]{1,0:T(8,128)}, f32[3072,128]{1,0:T(8,128)}) fusion(s32[128]{0:T(128)S(1)} %get-tuple-element.56), kind=kLoop, calls=%fused_computation.90 | loop fusion | flops 3538944 | bytes 3146240 | tf_op jit(solution)/shard_map/cos | solution.py:46
  54.2 56.8 %all-to-all-done = f32[96,8,1536]{2,1,0:T(8,128)} async-done(((f32[96,8,1536]{2,1,0:T(8,128)}), f32[96,8,1536]{2,1,0:T(8,128)}, u32[]{:S(2)}, u32[]{:S(2)}) %all-to-all-start) | async-done | bytes 4718624 | tf_op jit(solution)/shard_map/all_to_all | solution.py:99
  118.1 5.4 %all-to-all-start.1 = ((f32[2,288,1536]{2,1,0:T(8,128)}), f32[2,288,1536]{2,1,0:T(8,128)}, u32[]{:S(2)}, u32[]{:S(2)}) async-start(f32[2,288,1536]{2,1,0:T(8,128)} %bitcast.67), calls=%async_computation.1 | async-start | bytes 7077888 | tf_op jit(solution)/shard_map/all_to_all | solution.py:83
  125.6 8.0 %fusion.39 = (f32[3072,128]{1,0:T(8,128)}, f32[3072,128]{1,0:T(8,128)}) fusion(s32[128]{0:T(128)} %get-tuple-element.55), kind=kLoop, calls=%fused_computation.85 | loop fusion | flops 3538944 | bytes 3146240 | tf_op jit(solution)/shard_map/cos | solution.py:46
  133.5 7.5 %fusion.35 = (f32[3072,128]{1,0:T(8,128)}, f32[3072,128]{1,0:T(8,128)}) fusion(s32[128]{0:T(128)S(1)} %get-tuple-element.54), kind=kLoop, calls=%fused_computation.80 | loop fusion | flops 3538944 | bytes 3146240 | tf_op jit(solution)/shard_map/cos | solution.py:46
  141.0 22.0 %all-to-all-done.1 = f32[2,288,1536]{2,1,0:T(8,128)} async-done(((f32[2,288,1536]{2,1,0:T(8,128)}), f32[2,288,1536]{2,1,0:T(8,128)}, u32[]{:S(2)}, u32[]{:S(2)}) %all-to-all-start.1) | async-done | bytes 3538976 | tf_op jit(solution)/shard_map/all_to_all | solution.py:83
  169.0 3.3 fusion.10
  172.4 3.0 fusion.73
  175.5 3.6 convolution_add_fusion.6
  182.2 3.4 convolution_add_fusion.5
  185.6 3.0 fusion.75
  188.7 3.8 convolution_add_fusion.4
  195.6 3.4 convolution_add_fusion.3
  199.0 3.0 fusion.77
  202.1 3.6 convolution_add_fusion.2
  205.7 3.0 fusion.78
  208.7 3.4 convolution_add_fusion.1
  212.1 3.3 fusion.79
  215.4 3.4 convolution_add_fusion
  220.8 5.5 %all-to-all-start.2 = ((f32[288,2,1536]{2,0,1:T(8,128)}), f32[288,2,1536]{2,0,1:T(8,128)}, u32[]{:S(2)}, u32[]{:S(2)}) async-start(f32[288,2,1536]{2,0,1:T(8,128)} %bitcast.68), calls=%async_computation.2 | async-start | bytes 7077888 | tf_op jit(solution)/shard_map/all_to_all | solution.py:86
  229.0 36.0 %all-to-all-done.2 = f32[288,2,1536]{2,0,1:T(8,128)} async-done(((f32[288,2,1536]{2,0,1:T(8,128)}), f32[288,2,1536]{2,0,1:T(8,128)}, u32[]{:S(2)}, u32[]{:S(2)}) %all-to-all-start.2) | async-done | bytes 3538976 | tf_op jit(solution)/shard_map/all_to_all | solution.py:86
  269.5 5.5 %copy.19 = f32[12,64,1536]{2,0,1:T(8,128)} copy(f32[12,64,1536]{2,1,0:T(8,128)S(1)} %pad_maximum_fusion) | data formatting | bytes 9437184 | tf_op jit(solution)/shard_map/concatenate | solution.py:109
  275.0 7.8 %all-to-all-start.3 = ((f32[12,64,1536]{2,0,1:T(8,128)}), f32[12,64,1536]{2,0,1:T(8,128)}, u32[]{:S(2)}, u32[]{:S(2)}) async-start(f32[12,64,1536]{2,0,1:T(8,128)} %copy.19), calls=%async_computation.3 | async-start | bytes 12582912 | tf_op jit(solution)/shard_map/all_to_all | solution.py:117
  283.1 137.9 %all-to-all-done.3 = f32[12,64,1536]{2,0,1:T(8,128)} async-done(((f32[12,64,1536]{2,0,1:T(8,128)}), f32[12,64,1536]{2,0,1:T(8,128)}, u32[]{:S(2)}, u32[]{:S(2)}) %all-to-all-start.3) | async-done | bytes 4718624 | tf_op jit(solution)/shard_map/all_to_all | solution.py:117
  421.0 5.5 %copy.21 = f32[8,12,8,1536]{3,2,1,0:T(8,128)S(1)} copy(f32[8,12,8,1536]{3,1,2,0:T(8,128)} %bitcast.10) | data formatting | bytes 9437184 | tf_op jit(solution)/shard_map/all_to_all | solution.py:117
  435.2 5.6 %collective-permute-done.1 = f32[2,32,8,1]{3,2,1,0:T(8,128)S(1)} collective-permute-done((f32[2,32,8,1]{3,2,1,0:T(8,128)S(1)}, f32[2,32,8,1]{3,2,1,0:T(8,128)S(1)}, u32[]{:S(2)}, u32[]{:S(2)}) %collective-permute-start.1) | collective-permute-done | bytes 2080 | tf_op jit(solution)/shard_map/ppermute | solution.py:22
  (127 shorter events, 49.3 us)
Async XLA Ops:
  0.0 9.3 %copy-start.27 = (s32[64]{0:T(128)S(1)}, s32[64]{0:T(128)}, u32[]{:S(2)}) copy-start(s32[64]{0:T(128)} %param.14) | copy-start | bytes 772
  0.0 111.0 %all-to-all-start = ((f32[96,8,1536]{2,1,0:T(8,128)}), f32[96,8,1536]{2,1,0:T(8,128)}, u32[]{:S(2)}, u32[]{:S(2)}) async-start(f32[96,8,1536]{2,1,0:T(8,128)} %bitcast.64), calls=%async_computation | async-start | bytes 9437184 | tf_op jit(solution)/shard_map/all_to_all | solution.py:99
  6.5 11.0 %copy-start.29 = (s32[128]{0:T(128)}, s32[128]{0:T(128)S(1)}, u32[]{:S(2)}) copy-start(s32[128]{0:T(128)S(1)} %iota_add_fusion.6) | copy-start | bytes 1540
  7.0 32.5 %copy-start.31 = (s32[128]{0:T(128)}, s32[128]{0:T(128)S(1)}, u32[]{:S(2)}) copy-start(s32[128]{0:T(128)S(1)} %get-tuple-element.57) | copy-start | bytes 1540
  7.0 39.8 %copy-start.30 = (s32[128]{0:T(128)}, s32[128]{0:T(128)S(1)}, u32[]{:S(2)}) copy-start(s32[128]{0:T(128)S(1)} %get-tuple-element.56) | copy-start | bytes 1540
  7.0 17.8 %copy-start.33 = (s32[128]{0:T(128)}, s32[128]{0:T(128)S(1)}, u32[]{:S(2)}) copy-start(s32[128]{0:T(128)S(1)} %get-tuple-element.59) | copy-start | bytes 1540
  7.1 25.2 %copy-start.32 = (s32[128]{0:T(128)}, s32[128]{0:T(128)S(1)}, u32[]{:S(2)}) copy-start(s32[128]{0:T(128)S(1)} %get-tuple-element.58) | copy-start | bytes 1540
  118.1 44.9 %all-to-all-start.1 = ((f32[2,288,1536]{2,1,0:T(8,128)}), f32[2,288,1536]{2,1,0:T(8,128)}, u32[]{:S(2)}, u32[]{:S(2)}) async-start(f32[2,288,1536]{2,1,0:T(8,128)} %bitcast.67), calls=%async_computation.1 | async-start | bytes 7077888 | tf_op jit(solution)/shard_map/all_to_all | solution.py:83
  175.4 3.6 copy-start.9
  175.4 3.6 copy-start.10
  175.4 3.6 copy-start.24
  182.1 3.4 copy-start.7
  182.1 3.4 copy-start.8
  182.2 3.4 copy-start.23
  188.6 3.9 copy-start.5
  188.6 3.9 copy-start.6
  188.6 3.9 copy-start.22
  202.0 3.6 copy-start.15
  202.0 3.6 copy-start.16
  202.0 3.6 copy-start.20
  220.8 5.5 %copy-start.28 = (s32[64]{0:T(128)S(1)}, s32[64]{0:T(128)}, u32[]{:S(2)}) copy-start(s32[64]{0:T(128)} %param.15) | copy-start | bytes 772
  220.8 44.1 %all-to-all-start.2 = ((f32[288,2,1536]{2,0,1:T(8,128)}), f32[288,2,1536]{2,0,1:T(8,128)}, u32[]{:S(2)}, u32[]{:S(2)}) async-start(f32[288,2,1536]{2,0,1:T(8,128)} %bitcast.68), calls=%async_computation.2 | async-start | bytes 7077888 | tf_op jit(solution)/shard_map/all_to_all | solution.py:86
  275.0 7.8 %copy-start.35 = (f32[64]{0:T(128)S(1)}, f32[64]{0:T(128)}, u32[]{:S(2)}) copy-start(f32[64]{0:T(128)} %param.11) | copy-start | bytes 772
  275.0 7.9 %copy-start.36 = (f32[64]{0:T(128)S(1)}, f32[64]{0:T(128)}, u32[]{:S(2)}) copy-start(f32[64]{0:T(128)} %param.10) | copy-start | bytes 772
  275.0 8.0 %copy-start.37 = (f32[64]{0:T(128)S(1)}, f32[64]{0:T(128)}, u32[]{:S(2)}) copy-start(f32[64]{0:T(128)} %param.12) | copy-start | bytes 772
  275.0 146.0 %all-to-all-start.3 = ((f32[12,64,1536]{2,0,1:T(8,128)}), f32[12,64,1536]{2,0,1:T(8,128)}, u32[]{:S(2)}, u32[]{:S(2)}) async-start(f32[12,64,1536]{2,0,1:T(8,128)} %copy.19), calls=%async_computation.3 | async-start | bytes 12582912 | tf_op jit(solution)/shard_map/all_to_all | solution.py:117
  428.1 7.0 %collective-permute-start = (f32[2,32,8,1]{3,2,1,0:T(8,128)S(1)}, f32[2,32,8,1]{3,2,1,0:T(8,128)S(1)}, u32[]{:S(2)}, u32[]{:S(2)}) collective-permute-start(f32[2,32,8,1]{3,2,1,0:T(8,128)S(1)} %get-tuple-element.16), channel_id=1, source_target_pairs={{0,1},{1,0},{2,3},{3,2},{4,5},{5,4},{6,7},{7,6},{8,9},{9,8},{10,11... | collective-permute-start | bytes 6152 | tf_op jit(solution)/shard_map/ppermute | solution.py:20
  428.2 12.6 %collective-permute-start.1 = (f32[2,32,8,1]{3,2,1,0:T(8,128)S(1)}, f32[2,32,8,1]{3,2,1,0:T(8,128)S(1)}, u32[]{:S(2)}, u32[]{:S(2)}) collective-permute-start(f32[2,32,8,1]{3,2,1,0:T(8,128)S(1)} %get-tuple-element.17), channel_id=1, source_target_pairs={{1,0},{0,1},{3,2},{2,3},{5,4},{4,5},{7,6},{6,7},{9,8},{8,9},{11,10... | collective-permute-start | bytes 6152 | tf_op jit(solution)/shard_map/ppermute | solution.py:22
  429.7 14.0 %slice-start = ((s8[4718592]{0:T(1024)(128)(4,1)}), s8[4194304]{0:T(1024)(128)(4,1)S(1)}, s32[]{:S(2)}) async-start(s8[4718592]{0:T(1024)(128)(4,1)} %bitcast.65), calls=%async_computation.4 | async-start | bytes 8388608
  430.1 12.4 %collective-permute-start.2 = (f32[2,32,1,1536]{3,2,1,0:T(1,128)S(1)}, f32[2,32,1,1536]{3,2,1,0:T(1,128)S(1)}, u32[]{:S(2)}, u32[]{:S(2)}) collective-permute-start(f32[2,32,1,1536]{3,2,1,0:T(1,128)S(1)} %get-tuple-element.18), channel_id=1, source_target_pairs={{0,2},{2,4},{4,6},{6,8},{8,10},{10,12},{12,14},{1,3},{3,5},{5,7},{... | collective-permute-start | bytes 1179656 | tf_op jit(solution)/shard_map/ppermute | solution.py:20
  432.3 11.4 %slice-start.1 = ((s8[4718592]{0:T(1024)(128)(4,1)}), s8[524288]{0:T(1024)(128)(4,1)S(1)}, s32[]{:S(2)}) async-start(s8[4718592]{0:T(1024)(128)(4,1)} %bitcast.65), calls=%async_computation.5 | async-start | bytes 1048576
  432.4 10.2 %collective-permute-start.3 = (f32[2,32,1,1536]{3,2,1,0:T(1,128)S(1)}, f32[2,32,1,1536]{3,2,1,0:T(1,128)S(1)}, u32[]{:S(2)}, u32[]{:S(2)}) collective-permute-start(f32[2,32,1,1536]{3,2,1,0:T(1,128)S(1)} %get-tuple-element.19), channel_id=1, source_target_pairs={{2,0},{4,2},{6,4},{8,6},{10,8},{12,10},{14,12},{3,1},{5,3},{7,5},{... | collective-permute-start | bytes 1179656 | tf_op jit(solution)/shard_map/ppermute | solution.py:22
  (16 other events, 44.9 us)
where the time goes:
time: 457 us; the launch traced here: 448 us
  waiting for transfers between devices  258 us (56%)
  other arithmetic  78.8 us (17%)
  matrix products  52.3 us (11%)
  starting transfers between devices  31.6 us (7%)
  local copies, waits for them, and re-layouts  26.1 us (6%)
    all_to_all x1, waiting for transfers between devices, on_device(): lax.all_to_all(bands, 'lat', split_axis=1, concat_axis=0, tiled=True)  138 us
    all_to_all x1, waiting for transfers between devices, on_device(): lax.all_to_all(stacked, 'lat', split_axis=0, concat_axis=1, tiled=True)  56.8 us
    cos x7, other arithmetic, wave_table(): return jnp.concatenate([jnp.cos(angle), jnp.sin(angle)], axis=1)  52.1 us
    all_to_all x1, waiting for transfers between devices, transpose_filter(): lax.all_to_all(smoothed, 'lon', split_axis=1, concat_axis=0, tiled=True)  36 us
    dot_general x8, matrix products, project_rows(): jnp.dot(coefs * weights, table.T, precision=lax.Precision.HIGHEST, prefer...  27.8 us
    dot_general x8, matrix products, project_rows(): jnp.dot(row_data, table, precision=lax.Precision.HIGHEST, preferred_eleme...  24.5 us
    all_to_all x1, waiting for transfers between devices, transpose_filter(): lax.all_to_all(row_data, 'lon', split_axis=0, concat_axis=1, tiled=True)  22 us
  transfers between devices with their start and end apart: 8, of which 6 were waited for; matrix products, arithmetic and copies ran while one was open for 16% of the time, Pallas kernels for 0%

commit v1 on v0

--- a/solution.py
+++ b/solution.py
@@ -1,8 +1,13 @@
+import functools
 import math
 
 import jax
 import jax.numpy as jnp
+import ml_dtypes
+import numpy as np
 from jax import lax
+from jax.experimental import pallas as pl
+from jax.experimental.pallas import tpu as pltpu
 from jax.sharding import PartitionSpec as P
 
 KMAX = 1024
@@ -143,9 +148,331 @@
     return jnp.stack([new_height, new_east, new_north])
 
 
+RANK = 60
+TILE = 256
+LANES = 128
+
+
+def halves(value):
+    high = value.astype(jnp.bfloat16)
+    return high, (value - high.astype(jnp.float32)).astype(jnp.bfloat16)
+
+
+def split_table(value):
+    high = np.asarray(value, np.float32).astype(ml_dtypes.bfloat16)
+    low = (np.asarray(value, np.float32) - high.astype(np.float32)).astype(ml_dtypes.bfloat16)
+    return high, low
+
+
+@functools.lru_cache(maxsize=None)
+def kernel_tables(cells):
+    circle = 2 * cells
+
+    def kernel(distance):
+        wave = circle * np.sin(np.pi * (distance % (2 * circle)) / circle)
+        return np.where(distance % circle == 0, 0.0, 1.0 / np.where(distance % circle == 0, 1.0, wave))
+
+    n = np.arange(cells)
+    rest = kernel(n[:, None] - n[None, :] - cells)
+    columns, rows = [], []
+    for _ in range(RANK):
+        i, j = divmod(int(np.argmax(np.abs(rest))), cells)
+        pivot = rest[i, j]
+        size = np.sqrt(abs(pivot))
+        u, v = rest[:, j] / pivot * size, rest[i, :] / size
+        columns.append(u)
+        rows.append(v)
+        rest = rest - u[:, None] * v[None, :]
+    project = np.stack(
+        rows
+        + [kernel(cells - 1 - n), kernel(0 - n), kernel(cells - 1 - n - cells), kernel(0 - n - cells)],
+        axis=1,
+    )
+    expand = np.zeros((64, cells))
+    expand[:RANK] = np.stack(columns)
+    band = kernel(np.arange(2 * cells)[None, :] - np.arange(LANES)[:, None] - cells)
+    return project, expand, band.astype(np.float32)
+
+
+def project_kernel(x_ref, trig_ref, mix_ref, edge_ref, depth_ref, table_ref, out_ref):
+    x = x_ref[...]
+    fields, levels, rows, cells = x.shape
+    cos, sin = trig_ref[0][None, None], trig_ref[1][None, None]
+
+    def spectrum(value):
+        high, low = halves(value.reshape(fields * levels * rows, cells))
+        total = jnp.dot(high, table_ref[...], preferred_element_type=jnp.float32)
+        total = total + jnp.dot(low, table_ref[...], preferred_element_type=jnp.float32)
+        total = total + pltpu.roll(total, 64, 1)
+        return total.reshape(fields, levels, rows, LANES)
+
+    z = mix_ref[0][None, None] * spectrum(x * cos) + mix_ref[1][None, None] * spectrum(x * sin)
+    lane = lax.broadcasted_iota(jnp.int32, (1, 1, rows, LANES), 3)
+    z = z + jnp.where(lane == RANK, edge_ref[0][None, None] * x[..., cells - 1 :], 0.0)
+    z = z + jnp.where(lane == RANK + 1, edge_ref[0][None, None] * x[..., :1], 0.0)
+    depth = depth_ref[...].astype(jnp.float32)
+    z = z + jnp.where(lane == 124, depth[None, :, :, cells - 1 :], 0.0)
+    z = z + jnp.where(lane == 125, depth[None, :, :, :1], 0.0)
+    out_ref[...] = z
+
+
+def local_kernel(x_ref, trig_ref, inner_ref, band_ref, y_ref, high_ref, low_ref, band_high, band_low, total_ref):
+    row = pl.program_id(0)
+    cells = trig_ref.shape[2] // 2
+    lines = cells // LANES * 8
+    count = x_ref.shape[0] // lines
+    blocks = cells // TILE
+
+    def strip(block):
+        return pl.ds(block * 8 + row, count, stride=lines)
+
+    for block in range(blocks):
+        x = jnp.concatenate([x_ref[strip(2 * block), :], x_ref[strip(2 * block + 1), :]], axis=1)
+        high, low = halves(x)
+        high_ref[pl.ds(block * count, count), :] = high
+        low_ref[pl.ds(block * count, count), :] = low
+    inner_cos, inner_sin = inner_ref[0, 0], inner_ref[0, 1]
+    for block in range(2 * cells // LANES):
+        at = pl.ds(block * LANES, LANES)
+        value = band_ref[:, at] * (trig_ref[0, 1:2, at] * inner_cos - trig_ref[0, 0:1, at] * inner_sin)
+        high, low = halves(value)
+        band_high[:, at] = high
+        band_low[:, at] = low
+    for shift in [0] + [s * e for e in range(1, blocks) for s in (1, -1)]:
+        first = cells + TILE * shift
+        weights = [
+            jnp.concatenate([band[:, first : first + TILE], band[:, first - LANES : first - LANES + TILE]], axis=0)
+            for band in (band_high, band_low)
+        ]
+        start, stop = max(0, -shift), min(blocks, blocks - shift)
+        source = pl.ds(start * count, (stop - start) * count)
+        target = pl.ds((start + shift) * count, (stop - start) * count)
+        value = jnp.dot(high_ref[source, :], weights[0], preferred_element_type=jnp.float32)
+        value = value + jnp.dot(low_ref[source, :], weights[0], preferred_element_type=jnp.float32)
+        value = value + jnp.dot(high_ref[source, :], weights[1], preferred_element_type=jnp.float32)
+        if shift == 0:
+            total_ref[target, :] = value
+        else:
+            total_ref[target, :] += value
+    for block in range(blocks):
+        total = total_ref[pl.ds(block * count, count), :]
+        y_ref[strip(2 * block), :] = total[:, :LANES]
+        y_ref[strip(2 * block + 1), :] = total[:, LANES:]
+
+
+def join_kernel(x_ref, y_ref, z_ref, trig_ref, coef_ref, depth_ref, expand_ref, q_ref, first_ref, last_ref):
+    fields, levels, rows, cells = x_ref.shape
+    high, low = halves(z_ref[...].reshape(fields * levels * rows, LANES))
+
+    def expanded(turn):
+        part = pl.ds(turn * cells, cells)
+        value = jnp.dot(high, expand_ref[0, :, part], preferred_element_type=jnp.float32)
+        value = value + jnp.dot(low, expand_ref[0, :, part], preferred_element_type=jnp.float32)
+        value = value + jnp.dot(high, expand_ref[1, :, part], preferred_element_type=jnp.float32)
+        return value.reshape(fields, levels, rows, cells)
+
+    coef = coef_ref[...]
+    q = y_ref[...] + coef[:, 3:4][None, None] * x_ref[...]
+    q = q + trig_ref[0][None, None] * expanded(0)
+    q = q + trig_ref[1][None, None] * expanded(1)
+    q_ref[...] = q
+    merid = coef[:, 1:2][None]
+    north = merid * q[2]
+    flux = merid * (depth_ref[...].astype(jnp.float32) * q[0])
+    for side, ref in ((0, first_ref), (rows - 1, last_ref)):
+        ref[0] = north[:, side, :]
+        ref[1] = flux[:, side, :]
+
+
+def stencil_kernel(weight_ref, x_ref, q_ref, depth_ref, coef_ref, before_ref, after_ref, rims_ref, out_ref, run_ref):
+    step = pl.program_id(0)
+    _, levels, rows, cells = x_ref.shape
+    coef = coef_ref[...]
+    zonal, merid, coriolis = coef[:, 0:1], coef[:, 1:2], coef[:, 2:3]
+    row = lax.broadcasted_iota(jnp.int32, (rows, cells), 0)
+    column = lax.broadcasted_iota(jnp.int32, (rows, cells), 1)
+
+    def zonal_adjoint(value, west, east):
+        left = jnp.where(column == 0, west, pltpu.roll(value, 1, 1))
+        right = jnp.where(column == cells - 1, east, pltpu.roll(value, cells - 1, 1))
+        return zonal * (left - right)
+
+    def merid_adjoint(value, before, after):
+        value = merid * value
+        up = jnp.where(row == 0, before, pltpu.roll(value, 1, 0))
+        down = jnp.where(row == rows - 1, after, pltpu.roll(value, rows - 1, 0))
+        return up - down
+
+    @pl.when(step == 0)
+    def _():
+        run_ref[...] = jnp.zeros_like(run_ref)
+
+    for level in range(levels):
+        height, east, north = q_ref[0, level], q_ref[1, level], q_ref[2, level]
+        flux = depth_ref[level].astype(jnp.float32) * height
+        rims = rims_ref[level]
+        line = pl.ds(level, 1)
+        run_ref[...] -= zonal_adjoint(east, rims[:, 0:1], rims[:, 1:2]) + merid_adjoint(
+            north, before_ref[0, line, :], after_ref[0, line, :]
+        )
+        out_ref[0, level] = x_ref[0, level] + weight_ref[step * levels + level] * run_ref[...]
+        out_ref[1, level] = x_ref[1, level] - zonal_adjoint(flux, rims[:, 2:3], rims[:, 3:4]) - coriolis * north
+        out_ref[2, level] = (
+            x_ref[2, level]
+            - merid_adjoint(flux, before_ref[1, line, :], after_ref[1, line, :])
+            + coriolis * east
+        )
+
+
+def whole(array):
+    shape = array.shape
+    return pl.BlockSpec(shape, lambda *_: (0,) * len(shape))
+
+
+def on_pair(adjoint, depth, zonal_coef, merid_coef, coriolis, layer_weight, cutoffs, polar_flags):
+    fields, level_count, rows, cells = adjoint.shape
+    circle = 2 * cells
+    lat_count = lax.axis_size("lat")
+    first_row = lax.axis_index("lat") * rows
+    project, expand, band = kernel_tables(cells)
+    project_high, project_low = split_table(project)
+    project_table = jnp.asarray(np.concatenate([project_high, project_low], axis=1))
+    nothing = np.zeros_like(expand)
+    expand_table = jnp.asarray(
+        np.stack(split_table(np.block([[expand, nothing], [nothing, expand]])))
+    )
+
+    def mine(values):
+        return lax.dynamic_slice_in_dim(values, first_row, rows)
+
+    cuts, flags = mine(cutoffs), mine(polar_flags)
+    kept = 2 * cuts + 1
+    offsets = lax.iota(jnp.int32, circle) - cells
+    phase = (kept[:, None] * offsets[None, :]) % (2 * circle)
+    angle = phase.astype(jnp.float32) * (math.pi / circle)
+    cos, sin = jnp.cos(angle), jnp.sin(angle)
+    on = (flags > 0).astype(jnp.float32)[:, None]
+    keep = jnp.where(flags > 0, kept.astype(jnp.float32) / circle, 1.0)[:, None]
+    sign = on * jnp.where(cuts % 2 == 0, -1.0, 1.0)[:, None]
+    own_cos, own_sin = cos[:, cells:], sin[:, cells:]
+    trig = jnp.stack([own_cos, own_sin])
+    cross = jnp.stack([sign * own_cos, sign * own_sin])
+    outer = jnp.stack([on * cos, on * sin], axis=1)
+    inner = jnp.stack([own_cos[:, :LANES], own_sin[:, :LANES]], axis=1)[..., None]
+    one, zero = jnp.ones((rows, RANK), jnp.float32), jnp.zeros((rows, RANK), jnp.float32)
+    blank = jnp.zeros((rows, 4), jnp.float32)
+    end_cos, end_sin = own_cos[:, cells - 1 :], own_sin[:, cells - 1 :]
+    start_cos, start_sin = own_cos[:, :1], own_sin[:, :1]
+    mix = jnp.stack(
+        [
+            jnp.concatenate(
+                [one, on * end_sin, on * start_sin, sign * end_cos, sign * start_cos, zero, blank], axis=1
+            ),
+            jnp.concatenate(
+                [zero, -on * end_cos, -on * start_cos, sign * end_sin, sign * start_sin, one, blank], axis=1
+            ),
+        ]
+    )
+    coef = jnp.concatenate(
+        [
+            mine(zonal_coef)[:, None],
+            mine(merid_coef)[:, None],
+            mine(coriolis)[:, None],
+            keep,
+            jnp.zeros((rows, LANES - 4), jnp.float32),
+        ],
+        axis=1,
+    )
+    edge = keep[None]
+
+    part = 8
+    steps = level_count // part
+    four = pl.BlockSpec((fields, part, rows, cells), lambda i: (0, i, 0, 0))
+    three = pl.BlockSpec((part, rows, cells), lambda i: (i, 0, 0))
+    code = pl.BlockSpec((fields, part, rows, LANES), lambda i: (0, i, 0, 0))
+    lines = pl.BlockSpec((2, part, cells), lambda i: (0, i, 0))
+    limit = pltpu.CompilerParams(vmem_limit_bytes=48 * 2**20)
+    count = fields * level_count * rows
+
+    z = pl.pallas_call(
+        project_kernel,
+        grid=(steps,),
+        in_specs=[four, whole(trig), whole(mix), whole(edge), three, whole(project_table)],
+        out_specs=code,
+        out_shape=jax.ShapeDtypeStruct((fields, level_count, rows, LANES), jnp.float32),
+        compiler_params=limit,
+    )(adjoint, trig, mix, edge, depth, project_table)
+    arrived = lax.ppermute(z, "lon", [(0, 1), (1, 0)])
+
+    tiles = (fields * level_count, rows, cells // LANES, LANES)
+    flat = adjoint.reshape(tiles).transpose(0, 2, 1, 3).reshape(-1, LANES)
+    strip = count // rows * cells // TILE
+    y = pl.pallas_call(
+        local_kernel,
+        grid=(rows,),
+        in_specs=[
+            whole(flat),
+            pl.BlockSpec((1, 2, circle), lambda i: (i, 0, 0)),
+            pl.BlockSpec((1, 2, LANES, 1), lambda i: (i, 0, 0, 0)),
+            whole(band),
+        ],
+        out_specs=whole(flat),
+        out_shape=jax.ShapeDtypeStruct(flat.shape, jnp.float32),
+        scratch_shapes=[
+            pltpu.VMEM((strip, TILE), jnp.bfloat16),
+            pltpu.VMEM((strip, TILE), jnp.bfloat16),
+            pltpu.VMEM((LANES, circle), jnp.bfloat16),
+            pltpu.VMEM((LANES, circle), jnp.bfloat16),
+            pltpu.VMEM((strip, TILE), jnp.float32),
+        ],
+        cost_estimate=pl.CostEstimate(
+            flops=6 * count * cells * cells, bytes_accessed=8 * count * cells, transcendentals=0
+        ),
+        compiler_params=limit,
+    )(flat, outer, inner, jnp.asarray(band))
+
+    y = y.reshape(tiles[0], tiles[2], rows, LANES).transpose(0, 2, 1, 3).reshape(adjoint.shape)
+    edges = jax.ShapeDtypeStruct((2, level_count, cells), jnp.float32)
+    q, first, last = pl.pallas_call(
+        join_kernel,
+        grid=(steps,),
+        in_specs=[four, four, code, whole(cross), whole(coef), three, whole(expand_table)],
+        out_specs=[four, lines, lines],
+        out_shape=[jax.ShapeDtypeStruct(adjoint.shape, jnp.float32), edges, edges],
+        compiler_params=limit,
+    )(adjoint, y, arrived, cross, coef, depth, expand_table)
+    before = lax.ppermute(last, "lat", [(i, i + 1) for i in range(lat_count - 1)])
+    after = lax.ppermute(first, "lat", [(i + 1, i) for i in range(lat_count - 1)])
+
+    rims = arrived[:2, ..., RANK : RANK + 2] + z[:2, ..., RANK + 2 : RANK + 4]
+    rims = jnp.concatenate([rims[1], rims[0] * arrived[0, ..., 124:126]], axis=-1)
+    return pl.pallas_call(
+        stencil_kernel,
+        grid=(steps,),
+        in_specs=[
+            pl.BlockSpec(memory_space=pltpu.SMEM),
+            four,
+            four,
+            three,
+            whole(coef),
+            lines,
+            lines,
+            pl.BlockSpec((part, rows, 4), lambda i: (i, 0, 0)),
+        ],
+        out_specs=four,
+        out_shape=jax.ShapeDtypeStruct(adjoint.shape, jnp.float32),
+        scratch_shapes=[pltpu.VMEM((rows, cells), jnp.float32)],
+        compiler_params=limit,
+    )(layer_weight, adjoint, q, depth, coef, before, after, rims)
+
+
+def plan_for(mesh):
+    return on_pair if mesh.shape["lon"] == 2 and mesh.shape["lev"] == 1 else on_device
+
+
 def solution(mesh):
     return jax.shard_map(
-        on_device,
+        plan_for(mesh),
         mesh=mesh,
         in_specs=(
             P("member", "lev", "lat", "lon"),

time: 457 us -> 73.5 us (0.16); the launches traced: 448 us -> 73 us
  waiting for transfers between devices: 258 us -> 6.75 us
  other arithmetic: 78.8 us -> 6.3 us
  matrix products: 52.3 us -> 0 us
  Pallas kernels: 0 us -> 44.5 us
  starting transfers between devices: 31.6 us -> 8.05 us
  local copies, waits for them, and re-layouts: 26.1 us -> 7.16 us
    all_to_all x4 -> x0, waiting for transfers between devices: 253 us -> none  [the longest x1 138 us: on_device(): lax.all_to_all(bands, 'lat', split_axis=1, concat_axis=0, tiled=True)]
    dot_general x16 -> x0, matrix products: 52.3 us -> none  [the longest x8 27.8 us: project_rows(): jnp.dot(coefs * weights, table.T, precision=lax.Precision.HIGHEST, prefer...]
    cos x7 -> x1, other arithmetic: 52.1 us -> 0.48 us  [on_pair(): cos, sin = (jnp.cos(angle), jnp.sin(angle))]
    pallas_call x0 -> x4, Pallas kernels: none -> 44.5 us  [the longest x1 23 us: on_pair(): pl.pallas_call(local_kernel, grid=(rows,), in_specs=[whole(flat), pl.Bloc...]
    all_to_all x4 -> x0, starting transfers between devices: 25.2 us -> none  [the longest x1 7.79 us: on_device(): lax.all_to_all(bands, 'lat', split_axis=1, concat_axis=0, tiled=True)]
    all_to_all x4 -> x0, local copies, waits for them, and re-layouts: 12.8 us -> none  [the longest x1 5.51 us: on_device(): lax.all_to_all(bands, 'lat', split_axis=1, concat_axis=0, tiled=True)]
    sin x1 -> x0, other arithmetic: 8.16 us -> none  [wave_table(): return jnp.concatenate([jnp.cos(angle), jnp.sin(angle)], axis=1)]
    concatenate x1 -> x3, local copies, waits for them, and re-layouts: 5.53 us -> 0.24 us  [the longest x1 0.08 us: on_pair(): jnp.concatenate([one, on * end_sin, on * start_sin, sign * end_cos, sign...]
  transfers between devices with their start and end apart: 8 -> 3, of which waited for: 6 -> 2; matrix products, arithmetic and copies ran while one was open for 16% -> 8% of each run, Pallas kernels for 0% -> 32%
where the time goes in v1:
time: 73.5 us; the launch traced here: 73 us
  Pallas kernels  44.5 us (61%)
  starting transfers between devices  8.05 us (11%)
  local copies, waits for them, and re-layouts  7.16 us (10%)
  waiting for transfers between devices  6.75 us (9%)
  other arithmetic  6.3 us (9%)
    pallas_call x1, Pallas kernels, on_pair(): pl.pallas_call(local_kernel, grid=(rows,), in_specs=[whole(flat), pl.Bloc...  23 us
    pallas_call x1, Pallas kernels, on_pair(): pl.pallas_call(join_kernel, grid=(steps,), in_specs=[four, four, code, wh...  8.75 us
    pallas_call x1, Pallas kernels, on_pair(): pl.pallas_call(stencil_kernel, grid=(steps,), in_specs=[pl.BlockSpec(memo...  7.2 us
    pallas_call x1, Pallas kernels, on_pair(): pl.pallas_call(project_kernel, grid=(steps,), in_specs=[four, whole(trig)...  5.56 us
    unnamed x20, local copies, waits for them, and re-layouts  4.78 us
    ppermute x1, waiting for transfers between devices, on_pair(): lax.ppermute(first, 'lat', [(i + 1, i) for i in range(lat_count - 1)])  4.4 us
    ppermute x1, starting transfers between devices, on_pair(): lax.ppermute(last, 'lat', [(i, i + 1) for i in range(lat_count - 1)])  4.03 us
    mul x1, other arithmetic, on_pair(): outer = jnp.stack([on * cos, on * sin], axis=1)  3.57 us
  transfers between devices with their start and end apart: 3, of which 2 were waited for; matrix products, arithmetic and copies ran while one was open for 8% of the time, Pallas kernels for 32%

profile of v1, /device:TPU:1, one launch (start us, length us, event | category | flops | bytes accessed | tf_op | source)
XLA Modules:
  0.0 73.0 jit_solution(1151160421778207910)
XLA Ops:
  0.0 0.8 %fusion.12 = (f32[8,1]{0,1:T(1,128)S(1)}, s32[8]{0:T(128)S(1)}, pred[8]{0:T(512)(128)(4,1)S(1)}) fusion(s32[64]{0:T(128)} %param.17, s32[]{:T(128)S(6)} %select_n.41, s32[64]{0:T(128)} %param.18), kind=kLoop, calls=%fused_computation.53 | loop fusion | flops 48 | bytes 140 | tf_op jit(solution)/shard_map/broadcast_in_dim | solution.py:355
  0.8 0.7 %fusion.13 = (f32[1,8,1]{1,2,0:T(1,128)S(1)}, f32[8,1]{0,1:T(1,128)S(1)}, f32[8]{0:T(128)S(1)}) fusion(pred[8]{0:T(512)(128)(4,1)S(1)} %get-tuple-element.13, s32[8]{0:T(128)S(1)} %get-tuple-element.12, s32[64]{0:T(128)} %param.17, s32[]{:T(128)S(6)} %select_n.41), kind=kLoop, calls=%fused_computation.54 | loop fusion | flops 152 | bytes 172 | tf_op jit(solution)/shard_map/broadcast_in_dim;broadcast_in_dim | solution.py:386
  1.5 0.1 copy.60
  1.6 0.1 copy.68.edge_ref
  1.7 0.1 copy.64
  1.8 0.1 copy.62
  1.8 0.5 fusion.8
  2.5 0.1 concatenate.12
  2.7 1.1 %copy-done.1 = bf16[32,8,1536]{2,1,0:T(8,128)(2,1)S(1)} copy-done((bf16[32,8,1536]{2,1,0:T(8,128)(2,1)S(1)}, bf16[32,8,1536]{2,1,0:T(8,128)(2,1)}, u32[]{:S(2)}) %copy-start.1) | copy-done | bytes 786456
  3.8 1.0 %copy-done.5 = bf16[1536,128]{1,0:T(8,128)(2,1)S(1)} copy-done((bf16[1536,128]{1,0:T(8,128)(2,1)S(1)}, bf16[1536,128]{1,0:T(8,128)(2,1)}, u32[]{:S(2)}) %copy-start.5) | copy-done | bytes 393240
  4.8 5.6 %shard_map.110 = f32[3,32,8,128]{3,2,1,0:T(8,128)S(1)} custom-call(f32[3,32,8,1536]{3,2,1,0:T(8,128)} %x_ref.5, f32[2,8,1536]{2,1,0:T(8,128)S(1)} %pad_maximum_fusion.2.trig_ref, f32[2,8,128]{2,1,0:T(8,128)S(1)} %pad_maximum_fusion.4.mix_ref, f32[1,8,1]{2,1,0:T(8,128)S(1)} %copy.68.edge_ref, bf16[32,8,1536]{2,1,0:T(8,128)(2,1)S(1)} %copy-done.1, ...), custom_call_target="tpu_custom_call" | custom-call | tf_op jit(solution)/shard_map/pallas_call | solution.py:397
  10.4 2.1 %collective-permute-start = (f32[3,32,8,128]{3,2,1,0:T(8,128)S(1)}, f32[3,32,8,128]{3,2,1,0:T(8,128)S(1)}, u32[]{:S(2)}, u32[]{:S(2)}) collective-permute-start(f32[3,32,8,128]{3,2,1,0:T(8,128)S(1)} %shard_map.110), channel_id=1, source_target_pairs={{0,1},{1,0},{2,3},{3,2},{4,5},{5,4},{6,7},{7,6},{8,9},{9,8},{10,11... | collective-permute-start | bytes 1179656 | tf_op jit(solution)/shard_map/ppermute | solution.py:405
  12.5 3.6 %cosine_multiply_fusion = (f32[8,1,3072]{2,1,0:T(1,128)S(1)}, f32[8,1,3072]{2,1,0:T(1,128)S(1)}) fusion(f32[8]{0:T(128)S(1)} %get-tuple-element.46, s32[3072]{0:T(1024)S(1)} %iota_add_fusion, s32[8]{0:T(128)S(1)} %get-tuple-element.12), kind=kLoop, calls=%fused_computation.20 | loop fusion | flops 270336 | bytes 208960 | tf_op jit(solution)/shard_map/mul | solution.py:360
  16.0 1.3 %copy.59.inner_ref = f32[8,2,128,1]{3,2,1,0:T(8,128)} copy(f32[8,2,128,1]{2,0,1,3:T(8,128)S(1)} %maximum_bitcast_fusion) | data formatting | bytes 16384 | tf_op jit(solution)/shard_map/broadcast_in_dim | solution.py:361
  17.4 0.2 pad_maximum_fusion.trig_ref
  17.6 1.2 %copy-done.4 = f32[8,2,128,1]{3,2,1,0:T(8,128)S(1)} copy-done((f32[8,2,128,1]{3,2,1,0:T(8,128)S(1)}, f32[8,2,128,1]{3,2,1,0:T(8,128)}, u32[]{:S(2)}) %copy-start.4) | copy-done | bytes 8216
  18.8 1.4 %copy-done.7 = f32[128,3072]{1,0:T(8,128)S(1)} copy-done((f32[128,3072]{1,0:T(8,128)S(1)}, f32[128,3072]{1,0:T(8,128)}, u32[]{:S(2)}) %copy-start.7) | copy-done | bytes 1572888
  20.2 23.0 %shard_map.109 = f32[9216,128]{1,0:T(8,128)} custom-call(f32[9216,128]{1,0:T(8,128)} %bitcast.45, f32[8,2,3072]{2,1,0:T(2,128)S(1)} %pad_maximum_fusion.trig_ref, f32[8,2,128,1]{3,2,1,0:T(8,128)S(1)} %copy-done.4, f32[128,3072]{1,0:T(8,128)S(1)} %copy-done.7), custom_call_target="tpu_custom_call" | custom-call | flops 10871635968 | bytes 9437184 | tf_op jit(solution)/shard_map/pallas_call | solution.py:410
  43.3 0.1 copy.72
  43.4 0.1 copy.71
  43.6 0.1 copy.69
  43.7 0.1 copy.70
  43.8 0.1 concatenate.14.coef_ref
  43.9 8.7 %shard_map.111 = (f32[3,32,8,1536]{3,2,1,0:T(8,128)}, f32[2,32,1536]{2,1,0:T(8,128)S(1)}, f32[2,32,1536]{2,1,0:T(8,128)S(1)}) custom-call(f32[3,32,8,1536]{3,2,1,0:T(8,128)} %x_ref.5, f32[3,32,8,1536]{3,2,1,0:T(8,128)} %bitcast.46, f32[3,32,8,128]{3,2,1,0:T(8,128)S(1)} %collective-permute-done.z_ref, f32[2,8,1536]{2,1,0:T(8,128)S(1)} %pad_maximum_fusion.3.trig_ref, ...), custom_call_target="tpu_custom_call" | custom-call | tf_op jit(solution)/shard_map/pallas_call | solution.py:436
  52.6 4.0 %collective-permute-start.1 = (f32[2,32,1536]{2,1,0:T(8,128)S(1)}, f32[2,32,1536]{2,1,0:T(8,128)S(1)}, u32[]{:S(2)}, u32[]{:S(2)}) collective-permute-start(f32[2,32,1536]{2,1,0:T(8,128)S(1)} %get-tuple-element.9), channel_id=1, source_target_pairs={{0,2},{2,4},{4,6},{6,8},{8,10},{10,12},{12,14},{1,3},{3,5},{5,7},{... | collective-permute-start | bytes 1179656 | tf_op jit(solution)/shard_map/ppermute | solution.py:444
  56.7 1.9 %collective-permute-start.2 = (f32[2,32,1536]{2,1,0:T(8,128)S(1)}, f32[2,32,1536]{2,1,0:T(8,128)S(1)}, u32[]{:S(2)}, u32[]{:S(2)}) collective-permute-start(f32[2,32,1536]{2,1,0:T(8,128)S(1)} %get-tuple-element.10), channel_id=1, source_target_pairs={{2,0},{4,2},{6,4},{8,6},{10,8},{12,10},{14,12},{3,1},{5,3},{7,5},{... | collective-permute-start | bytes 1179656 | tf_op jit(solution)/shard_map/ppermute | solution.py:445
  58.6 0.2 slice_add_fusion
  58.8 0.1 slice_bitcast_fusion
  58.9 0.1 pad_maximum_fusion.1.rims_ref
  59.0 2.4 %collective-permute-done.1.before_ref = f32[2,32,1536]{2,1,0:T(8,128)S(1)} collective-permute-done((f32[2,32,1536]{2,1,0:T(8,128)S(1)}, f32[2,32,1536]{2,1,0:T(8,128)S(1)}, u32[]{:S(2)}, u32[]{:S(2)}) %collective-permute-start.1) | collective-permute-done | bytes 393248 | tf_op jit(solution)/shard_map/ppermute | solution.py:444
  61.4 4.4 %collective-permute-done.2.after_ref = f32[2,32,1536]{2,1,0:T(8,128)S(1)} collective-permute-done((f32[2,32,1536]{2,1,0:T(8,128)S(1)}, f32[2,32,1536]{2,1,0:T(8,128)S(1)}, u32[]{:S(2)}, u32[]{:S(2)}) %collective-permute-start.2) | collective-permute-done | bytes 393248 | tf_op jit(solution)/shard_map/ppermute | solution.py:445
  65.8 7.2 %shard_map.112 = f32[3,32,8,1536]{3,2,1,0:T(8,128)} custom-call(f32[32]{0:T(128)S(1)} %copy-done.6, f32[3,32,8,1536]{3,2,1,0:T(8,128)} %x_ref.5, f32[3,32,8,1536]{3,2,1,0:T(8,128)} %get-tuple-element.8.q_ref, bf16[32,8,1536]{2,1,0:T(8,128)(2,1)S(1)} %copy-done.2, f32[8,128]{1,0:T(8,128)S(1)} %concatenate.14.coef_ref, ...), custom_call_target="tpu_custom_call" | custom-call | tf_op jit(solution)/shard_map/pallas_call | solution.py:449
  (33 shorter events, 0.5 us)
Async XLA Ops:
  0.0 43.5 %copy-start = (f32[64]{0:T(128)S(1)}, f32[64]{0:T(128)}, u32[]{:S(2)}) copy-start(f32[64]{0:T(128)} %param.13) | copy-start | bytes 772
  2.7 1.1 %copy-start.1 = (bf16[32,8,1536]{2,1,0:T(8,128)(2,1)S(1)}, bf16[32,8,1536]{2,1,0:T(8,128)(2,1)}, u32[]{:S(2)}) copy-start(bf16[32,8,1536]{2,1,0:T(8,128)(2,1)} %depth_ref.5) | copy-start | bytes 2359300
  3.8 1.0 %copy-start.5 = (bf16[1536,128]{1,0:T(8,128)(2,1)S(1)}, bf16[1536,128]{1,0:T(8,128)(2,1)}, u32[]{:S(2)}) copy-start(bf16[1536,128]{1,0:T(8,128)(2,1)} %constant.64.clone.table_ref) | copy-start | bytes 1179652
  10.4 33.5 %collective-permute-start = (f32[3,32,8,128]{3,2,1,0:T(8,128)S(1)}, f32[3,32,8,128]{3,2,1,0:T(8,128)S(1)}, u32[]{:S(2)}, u32[]{:S(2)}) collective-permute-start(f32[3,32,8,128]{3,2,1,0:T(8,128)S(1)} %shard_map.110), channel_id=1, source_target_pairs={{0,1},{1,0},{2,3},{3,2},{4,5},{5,4},{6,7},{7,6},{8,9},{9,8},{10,11... | collective-permute-start | bytes 1179656 | tf_op jit(solution)/shard_map/ppermute | solution.py:405
  17.6 1.2 %copy-start.4 = (f32[8,2,128,1]{3,2,1,0:T(8,128)S(1)}, f32[8,2,128,1]{3,2,1,0:T(8,128)}, u32[]{:S(2)}) copy-start(f32[8,2,128,1]{3,2,1,0:T(8,128)} %copy.59.inner_ref) | copy-start | bytes 24580
  18.8 1.4 %copy-start.7 = (f32[128,3072]{1,0:T(8,128)S(1)}, f32[128,3072]{1,0:T(8,128)}, u32[]{:S(2)}) copy-start(f32[128,3072]{1,0:T(8,128)} %constant.66.clone.band_ref) | copy-start | bytes 4718596
  20.2 23.1 %copy-start.8 = (f32[64]{0:T(128)S(1)}, f32[64]{0:T(128)}, u32[]{:S(2)}) copy-start(f32[64]{0:T(128)} %param.15) | copy-start | bytes 772
  20.2 23.1 %copy-start.9 = (f32[64]{0:T(128)S(1)}, f32[64]{0:T(128)}, u32[]{:S(2)}) copy-start(f32[64]{0:T(128)} %param.14) | copy-start | bytes 772
  20.2 23.6 %copy-start.2 = (bf16[32,8,1536]{2,1,0:T(8,128)(2,1)S(1)}, bf16[32,8,1536]{2,1,0:T(8,128)(2,1)}, u32[]{:S(2)}) copy-start(bf16[32,8,1536]{2,1,0:T(8,128)(2,1)} %depth_ref.5) | copy-start | bytes 2359300
  20.2 23.6 %copy-start.3 = (bf16[2,128,3072]{2,1,0:T(8,128)(2,1)S(1)}, bf16[2,128,3072]{2,1,0:T(8,128)(2,1)}, u32[]{:S(2)}) copy-start(bf16[2,128,3072]{2,1,0:T(8,128)(2,1)} %constant.65.clone.expand_ref) | copy-start | bytes 4718596
  43.9 21.9 %copy-start.6 = (f32[32]{0:T(128)S(1)}, f32[32]{0:T(128)}, u32[]{:S(2)}) copy-start(f32[32]{0:T(128)} %weight_ref.1) | copy-start | bytes 388
  52.6 8.7 %collective-permute-start.1 = (f32[2,32,1536]{2,1,0:T(8,128)S(1)}, f32[2,32,1536]{2,1,0:T(8,128)S(1)}, u32[]{:S(2)}, u32[]{:S(2)}) collective-permute-start(f32[2,32,1536]{2,1,0:T(8,128)S(1)} %get-tuple-element.9), channel_id=1, source_target_pairs={{0,2},{2,4},{4,6},{6,8},{8,10},{10,12},{12,14},{1,3},{3,5},{5,7},{... | collective-permute-start | bytes 1179656 | tf_op jit(solution)/shard_map/ppermute | solution.py:444
  56.7 9.1 %collective-permute-start.2 = (f32[2,32,1536]{2,1,0:T(8,128)S(1)}, f32[2,32,1536]{2,1,0:T(8,128)S(1)}, u32[]{:S(2)}, u32[]{:S(2)}) collective-permute-start(f32[2,32,1536]{2,1,0:T(8,128)S(1)} %get-tuple-element.10), channel_id=1, source_target_pairs={{2,0},{4,2},{6,4},{8,6},{10,8},{12,10},{14,12},{3,1},{5,3},{7,5},{... | collective-permute-start | bytes 1179656 | tf_op jit(solution)/shard_map/ppermute | solution.py:445

commit v2 on v1

--- a/solution.py
+++ b/solution.py
@@ -216,29 +216,41 @@
     out_ref[...] = z
 
 
-def local_kernel(x_ref, trig_ref, inner_ref, band_ref, y_ref, high_ref, low_ref, band_high, band_low, total_ref):
-    row = pl.program_id(0)
+def local_row(row, x_ref, trig_ref, coef_ref, band_ref, high_ref, low_ref, band_high, band_low, total_ref):
     cells = trig_ref.shape[2] // 2
     lines = cells // LANES * 8
     count = x_ref.shape[0] // lines
     blocks = cells // TILE
+    chosen = lax.broadcasted_iota(jnp.int32, (8, LANES), 0) == row
+
+    def line(values):
+        return jnp.sum(jnp.where(chosen, values, 0.0), axis=0, keepdims=True)
 
     def strip(block):
         return pl.ds(block * 8 + row, count, stride=lines)
 
+    coef = line(coef_ref[...])
+    keep = coef[:, 3:4]
     for block in range(blocks):
         x = jnp.concatenate([x_ref[strip(2 * block), :], x_ref[strip(2 * block + 1), :]], axis=1)
         high, low = halves(x)
-        high_ref[pl.ds(block * count, count), :] = high
-        low_ref[pl.ds(block * count, count), :] = low
-    inner_cos, inner_sin = inner_ref[0, 0], inner_ref[0, 1]
+        at = pl.ds(block * count, count)
+        high_ref[at, :] = high
+        low_ref[at, :] = low
+        total_ref[at, :] = keep * x
+
+    def upright(which):
+        values = coef[:, 4:5] * line(trig_ref[which, :, cells : cells + LANES])
+        return jnp.broadcast_to(values, (LANES, LANES)).T
+
+    inner_cos, inner_sin = upright(0), upright(1)
     for block in range(2 * cells // LANES):
         at = pl.ds(block * LANES, LANES)
-        value = band_ref[:, at] * (trig_ref[0, 1:2, at] * inner_cos - trig_ref[0, 0:1, at] * inner_sin)
+        value = band_ref[:, at] * (line(trig_ref[1, :, at]) * inner_cos - line(trig_ref[0, :, at]) * inner_sin)
         high, low = halves(value)
         band_high[:, at] = high
         band_low[:, at] = low
-    for shift in [0] + [s * e for e in range(1, blocks) for s in (1, -1)]:
+    for shift in range(1 - blocks, blocks):
         first = cells + TILE * shift
         weights = [
             jnp.concatenate([band[:, first : first + TILE], band[:, first - LANES : first - LANES + TILE]], axis=0)
@@ -250,47 +262,77 @@
         value = jnp.dot(high_ref[source, :], weights[0], preferred_element_type=jnp.float32)
         value = value + jnp.dot(low_ref[source, :], weights[0], preferred_element_type=jnp.float32)
         value = value + jnp.dot(high_ref[source, :], weights[1], preferred_element_type=jnp.float32)
-        if shift == 0:
-            total_ref[target, :] = value
-        else:
-            total_ref[target, :] += value
-    for block in range(blocks):
-        total = total_ref[pl.ds(block * count, count), :]
-        y_ref[strip(2 * block), :] = total[:, :LANES]
-        y_ref[strip(2 * block + 1), :] = total[:, LANES:]
-
-
-def join_kernel(x_ref, y_ref, z_ref, trig_ref, coef_ref, depth_ref, expand_ref, q_ref, first_ref, last_ref):
+        total_ref[target, :] += value
+
+
+def rim_kernel(x_ref, trig_ref, coef_ref, band_ref, y_ref, *scratch):
+    local_row(pl.program_id(0) * 7, x_ref, trig_ref, coef_ref, band_ref, *scratch)
+    total_ref = scratch[-1]
+    count = y_ref.shape[1]
+    for block in range(y_ref.shape[2] // TILE):
+        y_ref[0, :, pl.ds(block * TILE, TILE)] = total_ref[pl.ds(block * count, count), :]
+
+
+def inner_kernel(x_ref, trig_ref, coef_ref, band_ref, rim_ref, sent_ref, y_ref, *scratch):
+    del sent_ref
+    row = pl.program_id(0)
+    _, count, cells = rim_ref.shape
+    lines = cells // LANES * 8
+    total_ref = scratch[-1]
+    is_rim = jnp.logical_or(row == 0, row == 7)
+
+    @pl.when(jnp.logical_not(is_rim))
+    def _():
+        local_row(row, x_ref, trig_ref, coef_ref, band_ref, *scratch)
+        for block in range(cells // LANES):
+            value = total_ref[pl.ds(block // 2 * count, count), pl.ds(block % 2 * LANES, LANES)]
+            y_ref[pl.ds(block * 8 + row, count, stride=lines), :] = value
+
+    @pl.when(is_rim)
+    def _():
+        for block in range(cells // LANES):
+            value = rim_ref[row // 7, :, pl.ds(block * LANES, LANES)]
+            y_ref[pl.ds(block * 8 + row, count, stride=lines), :] = value
+
+
+def expanded(z, expand_ref, part):
+    high, low = halves(z)
+    value = jnp.dot(high, expand_ref[0, :, part], preferred_element_type=jnp.float32)
+    value = value + jnp.dot(low, expand_ref[0, :, part], preferred_element_type=jnp.float32)
+    return value + jnp.dot(high, expand_ref[1, :, part], preferred_element_type=jnp.float32)
+
+
+def border_kernel(z_ref, y_ref, trig_ref, coef_ref, depth_ref, expand_ref, first_ref, last_ref):
+    _, count, cells = y_ref.shape
+    levels = depth_ref.shape[0]
+    depth = depth_ref[...].astype(jnp.float32)
+    for turn, row, ref in ((0, 0, first_ref), (1, 7, last_ref)):
+        z = z_ref[pl.ds(row, count, stride=8), :]
+        q = y_ref[turn]
+        q = q + trig_ref[0, row : row + 1] * expanded(z, expand_ref, pl.ds(0, cells))
+        q = q + trig_ref[1, row : row + 1] * expanded(z, expand_ref, pl.ds(cells, cells))
+        merid = coef_ref[row : row + 1, 1:2]
+        ref[0] = merid * q[2 * levels :]
+        ref[1] = merid * (depth[:, row, :] * q[:levels])
+
+
+def final_kernel(
+    weight_ref, x_ref, y_ref, z_ref, trig_ref, coef_ref, depth_ref, expand_ref, before_ref, after_ref, rims_ref,
+    out_ref, q_ref, run_ref,
+):
+    step = pl.program_id(0)
     fields, levels, rows, cells = x_ref.shape
-    high, low = halves(z_ref[...].reshape(fields * levels * rows, LANES))
-
-    def expanded(turn):
-        part = pl.ds(turn * cells, cells)
-        value = jnp.dot(high, expand_ref[0, :, part], preferred_element_type=jnp.float32)
-        value = value + jnp.dot(low, expand_ref[0, :, part], preferred_element_type=jnp.float32)
-        value = value + jnp.dot(high, expand_ref[1, :, part], preferred_element_type=jnp.float32)
-        return value.reshape(fields, levels, rows, cells)
-
-    coef = coef_ref[...]
-    q = y_ref[...] + coef[:, 3:4][None, None] * x_ref[...]
-    q = q + trig_ref[0][None, None] * expanded(0)
-    q = q + trig_ref[1][None, None] * expanded(1)
-    q_ref[...] = q
-    merid = coef[:, 1:2][None]
-    north = merid * q[2]
-    flux = merid * (depth_ref[...].astype(jnp.float32) * q[0])
-    for side, ref in ((0, first_ref), (rows - 1, last_ref)):
-        ref[0] = north[:, side, :]
-        ref[1] = flux[:, side, :]
-
-
-def stencil_kernel(weight_ref, x_ref, q_ref, depth_ref, coef_ref, before_ref, after_ref, rims_ref, out_ref, run_ref):
-    step = pl.program_id(0)
-    _, levels, rows, cells = x_ref.shape
     coef = coef_ref[...]
     zonal, merid, coriolis = coef[:, 0:1], coef[:, 1:2], coef[:, 2:3]
     row = lax.broadcasted_iota(jnp.int32, (rows, cells), 0)
     column = lax.broadcasted_iota(jnp.int32, (rows, cells), 1)
+
+    z = z_ref[...].reshape(fields * levels * rows, LANES)
+    q = y_ref[...]
+    for turn in range(2):
+        value = expanded(z, expand_ref, pl.ds(turn * cells, cells))
+        q = q + trig_ref[turn][None, None] * value.reshape(fields, levels, rows, cells)
+    q_ref[...] = q
 
     def zonal_adjoint(value, west, east):
         left = jnp.where(column == 0, west, pltpu.roll(value, 1, 1))
@@ -357,8 +399,7 @@
     own_cos, own_sin = cos[:, cells:], sin[:, cells:]
     trig = jnp.stack([own_cos, own_sin])
     cross = jnp.stack([sign * own_cos, sign * own_sin])
-    outer = jnp.stack([on * cos, on * sin], axis=1)
-    inner = jnp.stack([own_cos[:, :LANES], own_sin[:, :LANES]], axis=1)[..., None]
+    around = jnp.stack([cos, sin])
     one, zero = jnp.ones((rows, RANK), jnp.float32), jnp.zeros((rows, RANK), jnp.float32)
     blank = jnp.zeros((rows, 4), jnp.float32)
     end_cos, end_sin = own_cos[:, cells - 1 :], own_sin[:, cells - 1 :]
@@ -379,7 +420,8 @@
             mine(merid_coef)[:, None],
             mine(coriolis)[:, None],
             keep,
-            jnp.zeros((rows, LANES - 4), jnp.float32),
+            on,
+            jnp.zeros((rows, LANES - 5), jnp.float32),
         ],
         axis=1,
     )
@@ -404,66 +446,93 @@
     )(adjoint, trig, mix, edge, depth, project_table)
     arrived = lax.ppermute(z, "lon", [(0, 1), (1, 0)])
 
-    tiles = (fields * level_count, rows, cells // LANES, LANES)
+    circles = fields * level_count
+    tiles = (circles, rows, cells // LANES, LANES)
     flat = adjoint.reshape(tiles).transpose(0, 2, 1, 3).reshape(-1, LANES)
-    strip = count // rows * cells // TILE
+    strip = circles * cells // TILE
+    scratch = [
+        pltpu.VMEM((strip, TILE), jnp.bfloat16),
+        pltpu.VMEM((strip, TILE), jnp.bfloat16),
+        pltpu.VMEM((LANES, circle), jnp.bfloat16),
+        pltpu.VMEM((LANES, circle), jnp.bfloat16),
+        pltpu.VMEM((strip, TILE), jnp.float32),
+    ]
+    band = jnp.asarray(band)
+
+    def cost(done):
+        return pl.CostEstimate(
+            flops=6 * done * circles * cells * cells, bytes_accessed=8 * count * cells, transcendentals=0
+        )
+
+    rim = pl.pallas_call(
+        rim_kernel,
+        grid=(2,),
+        in_specs=[whole(flat), whole(around), whole(coef), whole(band)],
+        out_specs=pl.BlockSpec((1, circles, cells), lambda i: (i, 0, 0)),
+        out_shape=jax.ShapeDtypeStruct((2, circles, cells), jnp.float32),
+        scratch_shapes=scratch,
+        cost_estimate=cost(2),
+        compiler_params=limit,
+    )(flat, around, coef, band)
+
+    sent = arrived.reshape(count, LANES)
+    edges = jax.ShapeDtypeStruct((2, level_count, cells), jnp.float32)
+    first, last = pl.pallas_call(
+        border_kernel,
+        grid=(1,),
+        in_specs=[whole(sent), whole(rim), whole(cross), whole(coef), whole(depth), whole(expand_table)],
+        out_specs=[whole(edges), whole(edges)],
+        out_shape=[edges, edges],
+        compiler_params=limit,
+    )(sent, rim, cross, coef, depth, expand_table)
+    before = lax.ppermute(last, "lat", [(i, i + 1) for i in range(lat_count - 1)])
+    after = lax.ppermute(first, "lat", [(i + 1, i) for i in range(lat_count - 1)])
+
     y = pl.pallas_call(
-        local_kernel,
+        inner_kernel,
         grid=(rows,),
         in_specs=[
             whole(flat),
-            pl.BlockSpec((1, 2, circle), lambda i: (i, 0, 0)),
-            pl.BlockSpec((1, 2, LANES, 1), lambda i: (i, 0, 0, 0)),
+            whole(around),
+            whole(coef),
             whole(band),
+            whole(rim),
+            pl.BlockSpec(memory_space=pl.ANY),
         ],
         out_specs=whole(flat),
         out_shape=jax.ShapeDtypeStruct(flat.shape, jnp.float32),
-        scratch_shapes=[
-            pltpu.VMEM((strip, TILE), jnp.bfloat16),
-            pltpu.VMEM((strip, TILE), jnp.bfloat16),
-            pltpu.VMEM((LANES, circle), jnp.bfloat16),
-            pltpu.VMEM((LANES, circle), jnp.bfloat16),
-            pltpu.VMEM((strip, TILE), jnp.float32),
-        ],
-        cost_estimate=pl.CostEstimate(
-            flops=6 * count * cells * cells, bytes_accessed=8 * count * cells, transcendentals=0
-        ),
+        scratch_shapes=scratch,
+        cost_estimate=cost(rows - 2),
         compiler_params=limit,
-    )(flat, outer, inner, jnp.asarray(band))
-
+    )(flat, around, coef, band, rim, first)
     y = y.reshape(tiles[0], tiles[2], rows, LANES).transpose(0, 2, 1, 3).reshape(adjoint.shape)
-    edges = jax.ShapeDtypeStruct((2, level_count, cells), jnp.float32)
-    q, first, last = pl.pallas_call(
-        join_kernel,
-        grid=(steps,),
-        in_specs=[four, four, code, whole(cross), whole(coef), three, whole(expand_table)],
-        out_specs=[four, lines, lines],
-        out_shape=[jax.ShapeDtypeStruct(adjoint.shape, jnp.float32), edges, edges],
-        compiler_params=limit,
-    )(adjoint, y, arrived, cross, coef, depth, expand_table)
-    before = lax.ppermute(last, "lat", [(i, i + 1) for i in range(lat_count - 1)])
-    after = lax.ppermute(first, "lat", [(i + 1, i) for i in range(lat_count - 1)])
 
     rims = arrived[:2, ..., RANK : RANK + 2] + z[:2, ..., RANK + 2 : RANK + 4]
     rims = jnp.concatenate([rims[1], rims[0] * arrived[0, ..., 124:126]], axis=-1)
     return pl.pallas_call(
-        stencil_kernel,
+        final_kernel,
         grid=(steps,),
         in_specs=[
             pl.BlockSpec(memory_space=pltpu.SMEM),
             four,
             four,
+            code,
+            whole(cross),
+            whole(coef),
             three,
-            whole(coef),
+            whole(expand_table),
             lines,
             lines,
             pl.BlockSpec((part, rows, 4), lambda i: (i, 0, 0)),
         ],
         out_specs=four,
         out_shape=jax.ShapeDtypeStruct(adjoint.shape, jnp.float32),
-        scratch_shapes=[pltpu.VMEM((rows, cells), jnp.float32)],
+        scratch_shapes=[
+            pltpu.VMEM((fields, part, rows, cells), jnp.float32),
+            pltpu.VMEM((rows, cells), jnp.float32),
+        ],
         compiler_params=limit,
-    )(layer_weight, adjoint, q, depth, coef, before, after, rims)
+    )(layer_weight, adjoint, y, arrived, cross, coef, depth, expand_table, before, after, rims)
 
 
 def plan_for(mesh):

time: 73.5 us -> 65.6 us (0.89)
  local copies, waits for them, and re-layouts: 7.16 us -> 3.2 us
  other arithmetic: 6.3 us -> 3.05 us
  waiting for transfers between devices: 6.75 us -> 5.05 us
    ppermute x1, waiting for transfers between devices: 4.4 us -> 0.01 us  [on_pair(): lax.ppermute(first, 'lat', [(i + 1, i) for i in range(lat_count - 1)])]
    mul x1, other arithmetic: 3.57 us -> 0.74 us  [on_pair(): sign = on * jnp.where(cuts % 2 == 0, -1.0, 1.0)[:, None]]
    unnamed x20 -> x18, local copies, waits for them, and re-layouts: 4.78 us -> 2.16 us
    ppermute x1, waiting for transfers between devices: 2.35 us -> 4.28 us  [on_pair(): lax.ppermute(last, 'lat', [(i, i + 1) for i in range(lat_count - 1)])]
    broadcast_in_dim x2 -> x1, local copies, waits for them, and re-layouts: 1.35 us -> 0.01 us  [on_pair(): jnp.zeros((rows, LANES - 5), jnp.float32)]
    ppermute x1, starting transfers between devices: 1.92 us -> 3.13 us  [on_pair(): lax.ppermute(first, 'lat', [(i + 1, i) for i in range(lat_count - 1)])]
    ppermute x1, waiting for transfers between devices: 0.01 us -> 0.77 us  [on_pair(): arrived = lax.ppermute(z, 'lon', [(0, 1), (1, 0)])]
    broadcast_in_dim x2 -> x0, other arithmetic: 0.76 us -> none  [the longest x1 0.75 us: on_pair(): keep = jnp.where(flags > 0, kept.astype(jnp.float32) / circle, 1.0)[:, None]]
  transfers between devices with their start and end apart: 3 -> 3, of which waited for: 2 -> 2; matrix products, arithmetic and copies ran while one was open for 8% -> 2% of each run, Pallas kernels for 32% -> 43%
where the time goes in v2:
time: 65.6 us; the launch traced here: 65.1 us
  Pallas kernels  45.1 us (69%)
  starting transfers between devices  8.59 us (13%)
  waiting for transfers between devices  5.05 us (8%)
  local copies, waits for them, and re-layouts  3.2 us (5%)
  other arithmetic  3.05 us (5%)
    pallas_call x1, Pallas kernels, on_pair(): pl.pallas_call(inner_kernel, grid=(rows,), in_specs=[whole(flat), whole(a...  21.2 us
    pallas_call x1, Pallas kernels, on_pair(): pl.pallas_call(final_kernel, grid=(steps,), in_specs=[pl.BlockSpec(memory...  10 us
    pallas_call x1, Pallas kernels, on_pair(): pl.pallas_call(rim_kernel, grid=(2,), in_specs=[whole(flat), whole(around...  6.94 us
    pallas_call x1, Pallas kernels, on_pair(): pl.pallas_call(project_kernel, grid=(steps,), in_specs=[four, whole(trig)...  5.67 us
    ppermute x1, waiting for transfers between devices, on_pair(): lax.ppermute(last, 'lat', [(i, i + 1) for i in range(lat_count - 1)])  4.28 us
    ppermute x1, starting transfers between devices, on_pair(): lax.ppermute(last, 'lat', [(i, i + 1) for i in range(lat_count - 1)])  3.35 us
    ppermute x1, starting transfers between devices, on_pair(): lax.ppermute(first, 'lat', [(i + 1, i) for i in range(lat_count - 1)])  3.13 us
    unnamed x18, local copies, waits for them, and re-layouts  2.16 us
  transfers between devices with their start and end apart: 3, of which 2 were waited for; matrix products, arithmetic and copies ran while one was open for 2% of the time, Pallas kernels for 43%

profile of v2, /device:TPU:1, one launch (start us, length us, event | category | flops | bytes accessed | tf_op | source)
XLA Modules:
  0.0 65.1 jit_solution(5005598681201499755)
XLA Ops:
  0.0 0.8 %fusion.17 = (f32[1,8,1]{1,2,0:T(1,128)S(1)}, pred[8]{0:T(512)(128)(4,1)S(1)}, s32[8]{0:T(128)S(1)}) fusion(s32[64]{0:T(128)} %param.18, s32[]{:T(128)S(6)} %select_n.41, s32[64]{0:T(128)} %param.17), kind=kLoop, calls=%fused_computation.54 | loop fusion | flops 48 | bytes 140 | tf_op jit(solution)/shard_map/broadcast_in_dim;broadcast_in_dim | solution.py:428
  0.8 0.7 %fusion.15 = (f32[8]{0:T(128)S(1)}, f32[8,1]{0,1:T(1,128)S(1)}, f32[8,1]{0,1:T(1,128)S(1)}) fusion(pred[8]{0:T(512)(128)(4,1)S(1)} %get-tuple-element.10, s32[64]{0:T(128)} %param.17, s32[]{:T(128)S(6)} %select_n.41, s32[8]{0:T(128)S(1)} %get-tuple-element.11), kind=kLoop, calls=%fused_computation.44 | loop fusion | flops 152 | bytes 172 | tf_op jit(solution)/shard_map/mul | solution.py:398
  1.5 0.1 copy.47
  1.6 0.1 copy.52
  1.7 0.1 copy.56.edge_ref
  1.8 0.1 copy.50
  1.9 0.5 fusion.8
  2.3 0.1 multiply_bitcast_fusion.1
  2.5 0.1 concatenate.13
  2.6 0.1 concatenate.14
  2.7 1.1 %copy-done.1 = bf16[32,8,1536]{2,1,0:T(8,128)(2,1)S(1)} copy-done((bf16[32,8,1536]{2,1,0:T(8,128)(2,1)S(1)}, bf16[32,8,1536]{2,1,0:T(8,128)(2,1)}, u32[]{:S(2)}) %copy-start.1) | copy-done | bytes 786456
  3.8 1.0 %copy-done.4 = bf16[1536,128]{1,0:T(8,128)(2,1)S(1)} copy-done((bf16[1536,128]{1,0:T(8,128)(2,1)S(1)}, bf16[1536,128]{1,0:T(8,128)(2,1)}, u32[]{:S(2)}) %copy-start.4) | copy-done | bytes 393240
  4.8 5.7 %shard_map.110 = f32[3,32,8,128]{3,2,1,0:T(8,128)S(1)} custom-call(f32[3,32,8,1536]{3,2,1,0:T(8,128)} %x_ref.3, f32[2,8,1536]{2,1,0:T(8,128)S(1)} %pad_maximum_fusion.2.trig_ref, f32[2,8,128]{2,1,0:T(8,128)S(1)} %pad_maximum_fusion.4.mix_ref, f32[1,8,1]{2,1,0:T(8,128)S(1)} %copy.56.edge_ref, bf16[32,8,1536]{2,1,0:T(8,128)(2,1)S(1)} %copy-done.1, ...), custom_call_target="tpu_custom_call" | custom-call | tf_op jit(solution)/shard_map/pallas_call | solution.py:439
  10.5 2.1 %collective-permute-start = (f32[3,32,8,128]{3,2,1,0:T(8,128)S(1)}, f32[3,32,8,128]{3,2,1,0:T(8,128)S(1)}, u32[]{:S(2)}, u32[]{:S(2)}) collective-permute-start(f32[3,32,8,128]{3,2,1,0:T(8,128)S(1)} %shard_map.110), channel_id=1, source_target_pairs={{0,1},{1,0},{2,3},{3,2},{4,5},{5,4},{6,7},{7,6},{8,9},{9,8},{10,11... | collective-permute-start | bytes 1179656 | tf_op jit(solution)/shard_map/ppermute | solution.py:447
  12.6 0.5 fusion.12
  13.1 0.1 dynamic-slice_bitcast_fusion.2
  13.3 0.1 copy.45
  13.3 0.1 copy.43
  13.4 0.1 copy.46
  13.5 0.1 copy.44
  13.6 0.1 concatenate.12.coef_ref
  13.7 6.9 %shard_map.109.y_ref.rim_ref = f32[2,96,1536]{2,1,0:T(8,128)S(1)} custom-call(f32[9216,128]{1,0:T(8,128)} %bitcast.41, f32[2,8,3072]{2,1,0:T(8,128)S(1)} %pad_maximum_fusion.trig_ref, f32[8,128]{1,0:T(8,128)S(1)} %concatenate.12.coef_ref, f32[128,3072]{1,0:T(8,128)S(1)} %copy-done.6), custom_call_target="tpu_custom_call" | custom-call | flops 2717908992 | bytes 9437184 | tf_op jit(solution)/shard_map/pallas_call | solution.py:467
  20.7 0.8 %collective-permute-done.z_ref = f32[3,32,8,128]{3,2,1,0:T(8,128)S(1)} collective-permute-done((f32[3,32,8,128]{3,2,1,0:T(8,128)S(1)}, f32[3,32,8,128]{3,2,1,0:T(8,128)S(1)}, u32[]{:S(2)}, u32[]{:S(2)}) %collective-permute-start) | collective-permute-done | bytes 393248 | tf_op jit(solution)/shard_map/ppermute | solution.py:447
  21.5 1.3 %shard_map.111 = (f32[2,32,1536]{2,1,0:T(8,128)S(1)}, f32[2,32,1536]{2,1,0:T(8,128)S(1)}) custom-call(f32[768,128]{1,0:T(8,128)S(1)} %bitcast.40, f32[2,96,1536]{2,1,0:T(8,128)S(1)} %shard_map.109.y_ref.rim_ref, f32[2,8,1536]{2,1,0:T(8,128)S(1)} %pad_maximum_fusion.3.trig_ref, f32[8,128]{1,0:T(8,128)S(1)} %concatenate.12.coef_ref, ...), custom_call_target="tpu_custom_call" | custom-call | tf_op jit(solution)/shard_map/pallas_call | solution.py:480
  22.7 3.1 %collective-permute-start.2 = (f32[2,32,1536]{2,1,0:T(8,128)S(1)}, f32[2,32,1536]{2,1,0:T(8,128)S(1)}, u32[]{:S(2)}, u32[]{:S(2)}) collective-permute-start(f32[2,32,1536]{2,1,0:T(8,128)S(1)} %get-tuple-element.7.sent_ref), channel_id=1, source_target_pairs={{2,0},{4,2},{6,4},{8,6},{10,8},{12,10},{14,12},{3,1},{5,3},{7,5},{... | collective-permute-start | bytes 1179656 | tf_op jit(solution)/shard_map/ppermute | solution.py:489
  25.9 21.2 %shard_map.112 = f32[9216,128]{1,0:T(8,128)} custom-call(f32[9216,128]{1,0:T(8,128)} %bitcast.42, f32[2,8,3072]{2,1,0:T(8,128)S(1)} %pad_maximum_fusion.trig_ref, f32[8,128]{1,0:T(8,128)S(1)} %concatenate.12.coef_ref, f32[128,3072]{1,0:T(8,128)S(1)} %copy-done.6, f32[2,96,1536]{2,1,0:T(8,128)S(1)} %shard_map.109.y_ref.rim_ref, ...), custom_call_target="tpu_custom_call" | custom-call | flops 8153726976 | bytes 9437184 | tf_op jit(solution)/shard_map/pallas_call | solution.py:491
  47.0 3.3 %collective-permute-start.1 = (f32[2,32,1536]{2,1,0:T(8,128)S(1)}, f32[2,32,1536]{2,1,0:T(8,128)S(1)}, u32[]{:S(2)}, u32[]{:S(2)}) collective-permute-start(f32[2,32,1536]{2,1,0:T(8,128)S(1)} %get-tuple-element.8), channel_id=1, source_target_pairs={{0,2},{2,4},{4,6},{6,8},{8,10},{10,12},{12,14},{1,3},{3,5},{5,7},{... | collective-permute-start | bytes 1179656 | tf_op jit(solution)/shard_map/ppermute | solution.py:488
  50.4 0.2 slice_add_fusion
  50.6 0.1 slice_bitcast_fusion
  50.7 0.1 pad_maximum_fusion.1.rims_ref
  50.8 4.3 %collective-permute-done.1.before_ref = f32[2,32,1536]{2,1,0:T(8,128)S(1)} collective-permute-done((f32[2,32,1536]{2,1,0:T(8,128)S(1)}, f32[2,32,1536]{2,1,0:T(8,128)S(1)}, u32[]{:S(2)}, u32[]{:S(2)}) %collective-permute-start.1) | collective-permute-done | bytes 393248 | tf_op jit(solution)/shard_map/ppermute | solution.py:488
  55.1 10.0 %shard_map.113 = f32[3,32,8,1536]{3,2,1,0:T(8,128)} custom-call(f32[32]{0:T(128)S(1)} %copy-done.5, f32[3,32,8,1536]{3,2,1,0:T(8,128)} %x_ref.3, f32[3,32,8,1536]{3,2,1,0:T(8,128)} %bitcast.43, f32[3,32,8,128]{3,2,1,0:T(8,128)S(1)} %collective-permute-done.z_ref, f32[2,8,1536]{2,1,0:T(8,128)S(1)} %pad_maximum_fusion.3.trig_ref, ...), custom_call_target="tpu_custom_call" | custom-call | tf_op jit(solution)/shard_map/pallas_call | solution.py:512
  (29 shorter events, 0.2 us)
Async XLA Ops:
  0.0 13.1 %copy-start = (f32[64]{0:T(128)S(1)}, f32[64]{0:T(128)}, u32[]{:S(2)}) copy-start(f32[64]{0:T(128)} %param.13) | copy-start | bytes 772
  0.0 13.2 %copy-start.7 = (f32[64]{0:T(128)S(1)}, f32[64]{0:T(128)}, u32[]{:S(2)}) copy-start(f32[64]{0:T(128)} %param.15) | copy-start | bytes 772
  0.0 13.2 %copy-start.8 = (f32[64]{0:T(128)S(1)}, f32[64]{0:T(128)}, u32[]{:S(2)}) copy-start(f32[64]{0:T(128)} %param.14) | copy-start | bytes 772
  2.7 1.1 %copy-start.1 = (bf16[32,8,1536]{2,1,0:T(8,128)(2,1)S(1)}, bf16[32,8,1536]{2,1,0:T(8,128)(2,1)}, u32[]{:S(2)}) copy-start(bf16[32,8,1536]{2,1,0:T(8,128)(2,1)} %depth_ref.5) | copy-start | bytes 2359300
  3.8 1.0 %copy-start.4 = (bf16[1536,128]{1,0:T(8,128)(2,1)S(1)}, bf16[1536,128]{1,0:T(8,128)(2,1)}, u32[]{:S(2)}) copy-start(bf16[1536,128]{1,0:T(8,128)(2,1)} %constant.64.clone.table_ref) | copy-start | bytes 1179652
  4.8 8.9 %copy-start.6 = (f32[128,3072]{1,0:T(8,128)S(1)}, f32[128,3072]{1,0:T(8,128)}, u32[]{:S(2)}) copy-start(f32[128,3072]{1,0:T(8,128)} %constant.66.clone.band_ref) | copy-start | bytes 4718596
  10.5 10.9 %collective-permute-start = (f32[3,32,8,128]{3,2,1,0:T(8,128)S(1)}, f32[3,32,8,128]{3,2,1,0:T(8,128)S(1)}, u32[]{:S(2)}, u32[]{:S(2)}) collective-permute-start(f32[3,32,8,128]{3,2,1,0:T(8,128)S(1)} %shard_map.110), channel_id=1, source_target_pairs={{0,1},{1,0},{2,3},{3,2},{4,5},{5,4},{6,7},{7,6},{8,9},{9,8},{10,11... | collective-permute-start | bytes 1179656 | tf_op jit(solution)/shard_map/ppermute | solution.py:447
  13.7 7.7 %copy-start.2 = (bf16[32,8,1536]{2,1,0:T(8,128)(2,1)S(1)}, bf16[32,8,1536]{2,1,0:T(8,128)(2,1)}, u32[]{:S(2)}) copy-start(bf16[32,8,1536]{2,1,0:T(8,128)(2,1)} %depth_ref.5) | copy-start | bytes 2359300
  13.7 7.7 %copy-start.3 = (bf16[2,128,3072]{2,1,0:T(8,128)(2,1)S(1)}, bf16[2,128,3072]{2,1,0:T(8,128)(2,1)}, u32[]{:S(2)}) copy-start(bf16[2,128,3072]{2,1,0:T(8,128)(2,1)} %constant.65.clone.expand_ref) | copy-start | bytes 4718596
  22.7 32.4 %copy-start.5 = (f32[32]{0:T(128)S(1)}, f32[32]{0:T(128)}, u32[]{:S(2)}) copy-start(f32[32]{0:T(128)} %weight_ref.1) | copy-start | bytes 388
  22.7 32.4 %collective-permute-start.2 = (f32[2,32,1536]{2,1,0:T(8,128)S(1)}, f32[2,32,1536]{2,1,0:T(8,128)S(1)}, u32[]{:S(2)}, u32[]{:S(2)}) collective-permute-start(f32[2,32,1536]{2,1,0:T(8,128)S(1)} %get-tuple-element.7.sent_ref), channel_id=1, source_target_pairs={{2,0},{4,2},{6,4},{8,6},{10,8},{12,10},{14,12},{3,1},{5,3},{7,5},{... | collective-permute-start | bytes 1179656 | tf_op jit(solution)/shard_map/ppermute | solution.py:489
  47.0 8.1 %collective-permute-start.1 = (f32[2,32,1536]{2,1,0:T(8,128)S(1)}, f32[2,32,1536]{2,1,0:T(8,128)S(1)}, u32[]{:S(2)}, u32[]{:S(2)}) collective-permute-start(f32[2,32,1536]{2,1,0:T(8,128)S(1)} %get-tuple-element.8), channel_id=1, source_target_pairs={{0,2},{2,4},{4,6},{6,8},{8,10},{10,12},{12,14},{1,3},{3,5},{5,7},{... | collective-permute-start | bytes 1179656 | tf_op jit(solution)/shard_map/ppermute | solution.py:488

commit v3 on v2

--- a/solution.py
+++ b/solution.py
@@ -216,7 +216,7 @@
     out_ref[...] = z
 
 
-def local_row(row, x_ref, trig_ref, coef_ref, band_ref, high_ref, low_ref, band_high, band_low, total_ref):
+def local_row(row, x_ref, trig_ref, coef_ref, band_ref, terms_ref, band_high, band_low, total_ref):
     cells = trig_ref.shape[2] // 2
     lines = cells // LANES * 8
     count = x_ref.shape[0] // lines
@@ -235,8 +235,7 @@
         x = jnp.concatenate([x_ref[strip(2 * block), :], x_ref[strip(2 * block + 1), :]], axis=1)
         high, low = halves(x)
         at = pl.ds(block * count, count)
-        high_ref[at, :] = high
-        low_ref[at, :] = low
+        terms_ref[at, :] = jnp.concatenate([high, low, high], axis=1)
         total_ref[at, :] = keep * x
 
     def upright(which):
@@ -252,16 +251,18 @@
         band_low[:, at] = low
     for shift in range(1 - blocks, blocks):
         first = cells + TILE * shift
-        weights = [
-            jnp.concatenate([band[:, first : first + TILE], band[:, first - LANES : first - LANES + TILE]], axis=0)
-            for band in (band_high, band_low)
-        ]
+        weights = jnp.concatenate(
+            [
+                table[:, from_ : from_ + TILE]
+                for table in (band_high, band_high, band_low)
+                for from_ in (first, first - LANES)
+            ],
+            axis=0,
+        )
         start, stop = max(0, -shift), min(blocks, blocks - shift)
         source = pl.ds(start * count, (stop - start) * count)
         target = pl.ds((start + shift) * count, (stop - start) * count)
-        value = jnp.dot(high_ref[source, :], weights[0], preferred_element_type=jnp.float32)
-        value = value + jnp.dot(low_ref[source, :], weights[0], preferred_element_type=jnp.float32)
-        value = value + jnp.dot(high_ref[source, :], weights[1], preferred_element_type=jnp.float32)
+        value = jnp.dot(terms_ref[source, :], weights, preferred_element_type=jnp.float32)
         total_ref[target, :] += value
 
 
@@ -273,8 +274,8 @@
         y_ref[0, :, pl.ds(block * TILE, TILE)] = total_ref[pl.ds(block * count, count), :]
 
 
-def inner_kernel(x_ref, trig_ref, coef_ref, band_ref, rim_ref, sent_ref, y_ref, *scratch):
-    del sent_ref
+def inner_kernel(x_ref, trig_ref, coef_ref, band_ref, rim_ref, sent_ref, ends_ref, y_ref, *scratch):
+    del sent_ref, ends_ref
     row = pl.program_id(0)
     _, count, cells = rim_ref.shape
     lines = cells // LANES * 8
@@ -295,11 +296,14 @@
             y_ref[pl.ds(block * 8 + row, count, stride=lines), :] = value
 
 
-def expanded(z, expand_ref, part):
-    high, low = halves(z)
-    value = jnp.dot(high, expand_ref[0, :, part], preferred_element_type=jnp.float32)
-    value = value + jnp.dot(low, expand_ref[0, :, part], preferred_element_type=jnp.float32)
-    return value + jnp.dot(high, expand_ref[1, :, part], preferred_element_type=jnp.float32)
+def expanded(z, table_ref):
+    turned = pltpu.roll(z, 64, 1)
+    first = lax.broadcasted_iota(jnp.int32, z.shape, 1) < 64
+    results = []
+    for twice in (jnp.where(first, z, turned), jnp.where(first, turned, z)):
+        terms = jnp.concatenate(halves(twice), axis=1)
+        results.append(jnp.dot(terms, table_ref[...], preferred_element_type=jnp.float32))
+    return results
 
 
 def border_kernel(z_ref, y_ref, trig_ref, coef_ref, depth_ref, expand_ref, first_ref, last_ref):
@@ -308,9 +312,8 @@
     depth = depth_ref[...].astype(jnp.float32)
     for turn, row, ref in ((0, 0, first_ref), (1, 7, last_ref)):
         z = z_ref[pl.ds(row, count, stride=8), :]
-        q = y_ref[turn]
-        q = q + trig_ref[0, row : row + 1] * expanded(z, expand_ref, pl.ds(0, cells))
-        q = q + trig_ref[1, row : row + 1] * expanded(z, expand_ref, pl.ds(cells, cells))
+        with_cos, with_sin = expanded(z, expand_ref)
+        q = y_ref[turn] + trig_ref[0, row : row + 1] * with_cos + trig_ref[1, row : row + 1] * with_sin
         merid = coef_ref[row : row + 1, 1:2]
         ref[0] = merid * q[2 * levels :]
         ref[1] = merid * (depth[:, row, :] * q[:levels])
@@ -329,8 +332,7 @@
 
     z = z_ref[...].reshape(fields * levels * rows, LANES)
     q = y_ref[...]
-    for turn in range(2):
-        value = expanded(z, expand_ref, pl.ds(turn * cells, cells))
+    for turn, value in enumerate(expanded(z, expand_ref)):
         q = q + trig_ref[turn][None, None] * value.reshape(fields, levels, rows, cells)
     q_ref[...] = q
 
@@ -379,9 +381,9 @@
     project, expand, band = kernel_tables(cells)
     project_high, project_low = split_table(project)
     project_table = jnp.asarray(np.concatenate([project_high, project_low], axis=1))
-    nothing = np.zeros_like(expand)
+    expand_high, expand_low = split_table(expand)
     expand_table = jnp.asarray(
-        np.stack(split_table(np.block([[expand, nothing], [nothing, expand]])))
+        np.concatenate([expand_high, expand_low, expand_high, np.zeros_like(expand_high)])
     )
 
     def mine(values):
@@ -451,8 +453,7 @@
     flat = adjoint.reshape(tiles).transpose(0, 2, 1, 3).reshape(-1, LANES)
     strip = circles * cells // TILE
     scratch = [
-        pltpu.VMEM((strip, TILE), jnp.bfloat16),
-        pltpu.VMEM((strip, TILE), jnp.bfloat16),
+        pltpu.VMEM((strip, 3 * TILE), jnp.bfloat16),
         pltpu.VMEM((LANES, circle), jnp.bfloat16),
         pltpu.VMEM((LANES, circle), jnp.bfloat16),
         pltpu.VMEM((strip, TILE), jnp.float32),
@@ -488,6 +489,9 @@
     before = lax.ppermute(last, "lat", [(i, i + 1) for i in range(lat_count - 1)])
     after = lax.ppermute(first, "lat", [(i + 1, i) for i in range(lat_count - 1)])
 
+    rims = arrived[:2, ..., RANK : RANK + 2] + z[:2, ..., RANK + 2 : RANK + 4]
+    rims = jnp.concatenate([rims[1], rims[0] * arrived[0, ..., 124:126]], axis=-1)
+
     y = pl.pallas_call(
         inner_kernel,
         grid=(rows,),
@@ -498,17 +502,16 @@
             whole(band),
             whole(rim),
             pl.BlockSpec(memory_space=pl.ANY),
+            pl.BlockSpec(memory_space=pl.ANY),
         ],
         out_specs=whole(flat),
         out_shape=jax.ShapeDtypeStruct(flat.shape, jnp.float32),
         scratch_shapes=scratch,
         cost_estimate=cost(rows - 2),
         compiler_params=limit,
-    )(flat, around, coef, band, rim, first)
+    )(flat, around, coef, band, rim, first, rims)
     y = y.reshape(tiles[0], tiles[2], rows, LANES).transpose(0, 2, 1, 3).reshape(adjoint.shape)
 
-    rims = arrived[:2, ..., RANK : RANK + 2] + z[:2, ..., RANK + 2 : RANK + 4]
-    rims = jnp.concatenate([rims[1], rims[0] * arrived[0, ..., 124:126]], axis=-1)
     return pl.pallas_call(
         final_kernel,
         grid=(steps,),

time: 65.6 us -> 59.5 us (0.907)
  waiting for transfers between devices: 5.05 us -> 0.77 us
  Pallas kernels: 45.1 us -> 43.4 us
    ppermute x1, waiting for transfers between devices: 4.28 us -> 0.01 us  [on_pair(): lax.ppermute(last, 'lat', [(i, i + 1) for i in range(lat_count - 1)])]
    pallas_call x1, Pallas kernels: 10 us -> 8.54 us  [on_pair(): pl.pallas_call(final_kernel, grid=(steps,), in_specs=[pl.BlockSpec(memory...]
    ppermute x1, starting transfers between devices: 3.35 us -> 4.57 us  [on_pair(): lax.ppermute(last, 'lat', [(i, i + 1) for i in range(lat_count - 1)])]
    ppermute x1, starting transfers between devices: 3.13 us -> 1.92 us  [on_pair(): lax.ppermute(first, 'lat', [(i + 1, i) for i in range(lat_count - 1)])]
  transfers between devices with their start and end apart: 3 -> 3, of which waited for: 2 -> 1; matrix products, arithmetic and copies ran while one was open for 2% -> 2% of each run, Pallas kernels for 43% -> 48%
where the time goes in v3:
time: 59.5 us; the launch traced here: 59.2 us
  Pallas kernels  43.4 us (73%)
  starting transfers between devices  8.6 us (14%)
  local copies, waits for them, and re-layouts  3.2 us (5%)
  other arithmetic  3.05 us (5%)
  waiting for transfers between devices  0.77 us (1%)
    pallas_call x1, Pallas kernels, on_pair(): pl.pallas_call(inner_kernel, grid=(rows,), in_specs=[whole(flat), whole(a...  21.4 us
    pallas_call x1, Pallas kernels, on_pair(): pl.pallas_call(final_kernel, grid=(steps,), in_specs=[pl.BlockSpec(memory...  8.54 us
    pallas_call x1, Pallas kernels, on_pair(): pl.pallas_call(rim_kernel, grid=(2,), in_specs=[whole(flat), whole(around...  6.94 us
    pallas_call x1, Pallas kernels, on_pair(): pl.pallas_call(project_kernel, grid=(steps,), in_specs=[four, whole(trig)...  5.67 us
    ppermute x1, starting transfers between devices, on_pair(): lax.ppermute(last, 'lat', [(i, i + 1) for i in range(lat_count - 1)])  4.57 us
    unnamed x18, local copies, waits for them, and re-layouts  2.16 us
    ppermute x1, starting transfers between devices, on_pair(): arrived = lax.ppermute(z, 'lon', [(0, 1), (1, 0)])  2.11 us
    ppermute x1, starting transfers between devices, on_pair(): lax.ppermute(first, 'lat', [(i + 1, i) for i in range(lat_count - 1)])  1.92 us
  transfers between devices with their start and end apart: 3, of which 1 were waited for; matrix products, arithmetic and copies ran while one was open for 2% of the time, Pallas kernels for 48%

profile of v3, /device:TPU:1, one launch (start us, length us, event | category | flops | bytes accessed | tf_op | source)
XLA Modules:
  0.0 59.2 jit_solution(11246072788868051281)
XLA Ops:
  0.0 0.8 %fusion.17 = (f32[1,8,1]{1,2,0:T(1,128)S(1)}, pred[8]{0:T(512)(128)(4,1)S(1)}, s32[8]{0:T(128)S(1)}) fusion(s32[64]{0:T(128)} %param.18, s32[]{:T(128)S(6)} %select_n.41, s32[64]{0:T(128)} %param.17), kind=kLoop, calls=%fused_computation.54 | loop fusion | flops 48 | bytes 140 | tf_op jit(solution)/shard_map/broadcast_in_dim;broadcast_in_dim | solution.py:430
  0.8 0.7 %fusion.15 = (f32[8]{0:T(128)S(1)}, f32[8,1]{0,1:T(1,128)S(1)}, f32[8,1]{0,1:T(1,128)S(1)}) fusion(pred[8]{0:T(512)(128)(4,1)S(1)} %get-tuple-element.10, s32[64]{0:T(128)} %param.17, s32[]{:T(128)S(6)} %select_n.41, s32[8]{0:T(128)S(1)} %get-tuple-element.11), kind=kLoop, calls=%fused_computation.44 | loop fusion | flops 152 | bytes 172 | tf_op jit(solution)/shard_map/mul | solution.py:400
  1.5 0.1 copy.48
  1.6 0.1 copy.53
  1.7 0.1 copy.57.edge_ref
  1.8 0.1 copy.51
  1.9 0.5 fusion.8
  2.3 0.1 multiply_bitcast_fusion.1
  2.4 0.1 slice_multiply_fusion.6
  2.5 0.1 concatenate.13
  2.6 0.1 concatenate.14
  2.7 1.1 %copy-done.1 = bf16[32,8,1536]{2,1,0:T(8,128)(2,1)S(1)} copy-done((bf16[32,8,1536]{2,1,0:T(8,128)(2,1)S(1)}, bf16[32,8,1536]{2,1,0:T(8,128)(2,1)}, u32[]{:S(2)}) %copy-start.1) | copy-done | bytes 786456
  3.8 1.0 %copy-done.4 = bf16[1536,128]{1,0:T(8,128)(2,1)S(1)} copy-done((bf16[1536,128]{1,0:T(8,128)(2,1)S(1)}, bf16[1536,128]{1,0:T(8,128)(2,1)}, u32[]{:S(2)}) %copy-start.4) | copy-done | bytes 393240
  4.8 5.7 %shard_map.110 = f32[3,32,8,128]{3,2,1,0:T(8,128)S(1)} custom-call(f32[3,32,8,1536]{3,2,1,0:T(8,128)} %x_ref.3, f32[2,8,1536]{2,1,0:T(8,128)S(1)} %pad_maximum_fusion.2.trig_ref, f32[2,8,128]{2,1,0:T(8,128)S(1)} %pad_maximum_fusion.4.mix_ref, f32[1,8,1]{2,1,0:T(8,128)S(1)} %copy.57.edge_ref, bf16[32,8,1536]{2,1,0:T(8,128)(2,1)S(1)} %copy-done.1, ...), custom_call_target="tpu_custom_call" | custom-call | tf_op jit(solution)/shard_map/pallas_call | solution.py:441
  10.5 2.1 %collective-permute-start = (f32[3,32,8,128]{3,2,1,0:T(8,128)S(1)}, f32[3,32,8,128]{3,2,1,0:T(8,128)S(1)}, u32[]{:S(2)}, u32[]{:S(2)}) collective-permute-start(f32[3,32,8,128]{3,2,1,0:T(8,128)S(1)} %shard_map.110), channel_id=1, source_target_pairs={{0,1},{1,0},{2,3},{3,2},{4,5},{5,4},{6,7},{7,6},{8,9},{9,8},{10,11... | collective-permute-start | bytes 1179656 | tf_op jit(solution)/shard_map/ppermute | solution.py:449
  12.6 0.5 fusion.12
  13.1 0.1 dynamic-slice_bitcast_fusion.2
  13.3 0.1 copy.46
  13.3 0.1 copy.44
  13.4 0.1 copy.47
  13.5 0.1 copy.45
  13.6 0.1 concatenate.12.coef_ref
  13.7 6.9 %shard_map.109.y_ref.rim_ref = f32[2,96,1536]{2,1,0:T(8,128)S(1)} custom-call(f32[9216,128]{1,0:T(8,128)} %bitcast.41, f32[2,8,3072]{2,1,0:T(8,128)S(1)} %pad_maximum_fusion.trig_ref, f32[8,128]{1,0:T(8,128)S(1)} %concatenate.12.coef_ref, f32[128,3072]{1,0:T(8,128)S(1)} %copy-done.6), custom_call_target="tpu_custom_call" | custom-call | flops 2717908992 | bytes 9437184 | tf_op jit(solution)/shard_map/pallas_call | solution.py:468
  20.7 0.8 %collective-permute-done.z_ref = f32[3,32,8,128]{3,2,1,0:T(8,128)S(1)} collective-permute-done((f32[3,32,8,128]{3,2,1,0:T(8,128)S(1)}, f32[3,32,8,128]{3,2,1,0:T(8,128)S(1)}, u32[]{:S(2)}, u32[]{:S(2)}) %collective-permute-start) | collective-permute-done | bytes 393248 | tf_op jit(solution)/shard_map/ppermute | solution.py:449
  21.5 0.8 %shard_map.111 = (f32[2,32,1536]{2,1,0:T(8,128)S(1)}, f32[2,32,1536]{2,1,0:T(8,128)S(1)}) custom-call(f32[768,128]{1,0:T(8,128)S(1)} %bitcast.40, f32[2,96,1536]{2,1,0:T(8,128)S(1)} %shard_map.109.y_ref.rim_ref, f32[2,8,1536]{2,1,0:T(8,128)S(1)} %pad_maximum_fusion.3.trig_ref, f32[8,128]{1,0:T(8,128)S(1)} %concatenate.12.coef_ref, ...), custom_call_target="tpu_custom_call" | custom-call | tf_op jit(solution)/shard_map/pallas_call | solution.py:481
  22.3 4.6 %collective-permute-start.1 = (f32[2,32,1536]{2,1,0:T(8,128)S(1)}, f32[2,32,1536]{2,1,0:T(8,128)S(1)}, u32[]{:S(2)}, u32[]{:S(2)}) collective-permute-start(f32[2,32,1536]{2,1,0:T(8,128)S(1)} %get-tuple-element.8), channel_id=1, source_target_pairs={{0,2},{2,4},{4,6},{6,8},{8,10},{10,12},{12,14},{1,3},{3,5},{5,7},{... | collective-permute-start | bytes 1179656 | tf_op jit(solution)/shard_map/ppermute | solution.py:489
  26.9 1.9 %collective-permute-start.2 = (f32[2,32,1536]{2,1,0:T(8,128)S(1)}, f32[2,32,1536]{2,1,0:T(8,128)S(1)}, u32[]{:S(2)}, u32[]{:S(2)}) collective-permute-start(f32[2,32,1536]{2,1,0:T(8,128)S(1)} %get-tuple-element.7.sent_ref), channel_id=1, source_target_pairs={{2,0},{4,2},{6,4},{8,6},{10,8},{12,10},{14,12},{3,1},{5,3},{7,5},{... | collective-permute-start | bytes 1179656 | tf_op jit(solution)/shard_map/ppermute | solution.py:490
  28.8 0.2 slice_add_fusion
  29.0 0.1 slice_bitcast_fusion
  29.1 0.1 pad_maximum_fusion.1.ends_ref.rims_ref
  29.2 21.4 %shard_map.112 = f32[9216,128]{1,0:T(8,128)} custom-call(f32[9216,128]{1,0:T(8,128)} %bitcast.42, f32[2,8,3072]{2,1,0:T(8,128)S(1)} %pad_maximum_fusion.trig_ref, f32[8,128]{1,0:T(8,128)S(1)} %concatenate.12.coef_ref, f32[128,3072]{1,0:T(8,128)S(1)} %copy-done.6, f32[2,96,1536]{2,1,0:T(8,128)S(1)} %shard_map.109.y_ref.rim_ref, ...), custom_call_target="tpu_custom_call" | custom-call | flops 8153726976 | bytes 9437184 | tf_op jit(solution)/shard_map/pallas_call | solution.py:495
  50.6 8.5 %shard_map.113 = f32[3,32,8,1536]{3,2,1,0:T(8,128)} custom-call(f32[32]{0:T(128)S(1)} %copy-done.5, f32[3,32,8,1536]{3,2,1,0:T(8,128)} %x_ref.3, f32[3,32,8,1536]{3,2,1,0:T(8,128)} %bitcast.43, f32[3,32,8,128]{3,2,1,0:T(8,128)S(1)} %collective-permute-done.z_ref, f32[2,8,1536]{2,1,0:T(8,128)S(1)} %pad_maximum_fusion.3.trig_ref, ...), custom_call_target="tpu_custom_call" | custom-call | tf_op jit(solution)/shard_map/pallas_call | solution.py:515
  (29 shorter events, 0.2 us)
Async XLA Ops:
  0.0 13.1 %copy-start = (f32[64]{0:T(128)S(1)}, f32[64]{0:T(128)}, u32[]{:S(2)}) copy-start(f32[64]{0:T(128)} %param.13) | copy-start | bytes 772
  0.0 13.2 %copy-start.7 = (f32[64]{0:T(128)S(1)}, f32[64]{0:T(128)}, u32[]{:S(2)}) copy-start(f32[64]{0:T(128)} %param.15) | copy-start | bytes 772
  0.0 13.2 %copy-start.8 = (f32[64]{0:T(128)S(1)}, f32[64]{0:T(128)}, u32[]{:S(2)}) copy-start(f32[64]{0:T(128)} %param.14) | copy-start | bytes 772
  2.7 1.1 %copy-start.1 = (bf16[32,8,1536]{2,1,0:T(8,128)(2,1)S(1)}, bf16[32,8,1536]{2,1,0:T(8,128)(2,1)}, u32[]{:S(2)}) copy-start(bf16[32,8,1536]{2,1,0:T(8,128)(2,1)} %depth_ref.5) | copy-start | bytes 2359300
  3.8 1.0 %copy-start.4 = (bf16[1536,128]{1,0:T(8,128)(2,1)S(1)}, bf16[1536,128]{1,0:T(8,128)(2,1)}, u32[]{:S(2)}) copy-start(bf16[1536,128]{1,0:T(8,128)(2,1)} %constant.64.clone.table_ref) | copy-start | bytes 1179652
  4.8 8.9 %copy-start.6 = (f32[128,3072]{1,0:T(8,128)S(1)}, f32[128,3072]{1,0:T(8,128)}, u32[]{:S(2)}) copy-start(f32[128,3072]{1,0:T(8,128)} %constant.66.clone.band_ref) | copy-start | bytes 4718596
  10.5 10.9 %collective-permute-start = (f32[3,32,8,128]{3,2,1,0:T(8,128)S(1)}, f32[3,32,8,128]{3,2,1,0:T(8,128)S(1)}, u32[]{:S(2)}, u32[]{:S(2)}) collective-permute-start(f32[3,32,8,128]{3,2,1,0:T(8,128)S(1)} %shard_map.110), channel_id=1, source_target_pairs={{0,1},{1,0},{2,3},{3,2},{4,5},{5,4},{6,7},{7,6},{8,9},{9,8},{10,11... | collective-permute-start | bytes 1179656 | tf_op jit(solution)/shard_map/ppermute | solution.py:449
  13.7 7.7 %copy-start.2 = (bf16[32,8,1536]{2,1,0:T(8,128)(2,1)S(1)}, bf16[32,8,1536]{2,1,0:T(8,128)(2,1)}, u32[]{:S(2)}) copy-start(bf16[32,8,1536]{2,1,0:T(8,128)(2,1)} %depth_ref.5) | copy-start | bytes 2359300
  13.7 7.7 %copy-start.3 = (bf16[256,1536]{1,0:T(8,128)(2,1)S(1)}, bf16[256,1536]{1,0:T(8,128)(2,1)}, u32[]{:S(2)}) copy-start(bf16[256,1536]{1,0:T(8,128)(2,1)} %constant.65.clone.expand_ref) | copy-start | bytes 2359300
  22.3 28.3 %collective-permute-start.1 = (f32[2,32,1536]{2,1,0:T(8,128)S(1)}, f32[2,32,1536]{2,1,0:T(8,128)S(1)}, u32[]{:S(2)}, u32[]{:S(2)}) collective-permute-start(f32[2,32,1536]{2,1,0:T(8,128)S(1)} %get-tuple-element.8), channel_id=1, source_target_pairs={{0,2},{2,4},{4,6},{6,8},{8,10},{10,12},{12,14},{1,3},{3,5},{5,7},{... | collective-permute-start | bytes 1179656 | tf_op jit(solution)/shard_map/ppermute | solution.py:489
  26.9 23.7 %collective-permute-start.2 = (f32[2,32,1536]{2,1,0:T(8,128)S(1)}, f32[2,32,1536]{2,1,0:T(8,128)S(1)}, u32[]{:S(2)}, u32[]{:S(2)}) collective-permute-start(f32[2,32,1536]{2,1,0:T(8,128)S(1)} %get-tuple-element.7.sent_ref), channel_id=1, source_target_pairs={{2,0},{4,2},{6,4},{8,6},{10,8},{12,10},{14,12},{3,1},{5,3},{7,5},{... | collective-permute-start | bytes 1179656 | tf_op jit(solution)/shard_map/ppermute | solution.py:490
  29.2 21.4 %copy-start.5 = (f32[32]{0:T(128)S(1)}, f32[32]{0:T(128)}, u32[]{:S(2)}) copy-start(f32[32]{0:T(128)} %weight_ref.1) | copy-start | bytes 388

commit v4 on v3

--- a/solution.py
+++ b/solution.py
@@ -243,13 +243,14 @@
         return jnp.broadcast_to(values, (LANES, LANES)).T
 
     inner_cos, inner_sin = upright(0), upright(1)
-    for block in range(2 * cells // LANES):
+    def build(block):
         at = pl.ds(block * LANES, LANES)
         value = band_ref[:, at] * (line(trig_ref[1, :, at]) * inner_cos - line(trig_ref[0, :, at]) * inner_sin)
         high, low = halves(value)
         band_high[:, at] = high
         band_low[:, at] = low
-    for shift in range(1 - blocks, blocks):
+
+    def multiply(shift):
         first = cells + TILE * shift
         weights = jnp.concatenate(
             [
@@ -265,35 +266,53 @@
         value = jnp.dot(terms_ref[source, :], weights, preferred_element_type=jnp.float32)
         total_ref[target, :] += value
 
+    builds = [functools.partial(build, block) for block in range(2 * cells // LANES)]
+    return builds, [functools.partial(multiply, shift) for shift in range(1 - blocks, blocks)]
+
+
+def local_pair(rows, *refs):
+    arrays, scratch = refs[:4], refs[4:]
+    builds, products = local_row(rows[0], *arrays, *scratch[:4])
+    for build in builds:
+        build()
+    later_builds, later_products = local_row(rows[1], *arrays, *scratch[4:])
+    for turn, product in enumerate(products):
+        product()
+        for build in later_builds[turn :: len(products)]:
+            build()
+    for product in later_products:
+        product()
+
 
 def rim_kernel(x_ref, trig_ref, coef_ref, band_ref, y_ref, *scratch):
-    local_row(pl.program_id(0) * 7, x_ref, trig_ref, coef_ref, band_ref, *scratch)
-    total_ref = scratch[-1]
+    local_pair((0, 7), x_ref, trig_ref, coef_ref, band_ref, *scratch)
     count = y_ref.shape[1]
-    for block in range(y_ref.shape[2] // TILE):
-        y_ref[0, :, pl.ds(block * TILE, TILE)] = total_ref[pl.ds(block * count, count), :]
+    for turn in range(2):
+        for block in range(y_ref.shape[2] // TILE):
+            y_ref[turn, :, pl.ds(block * TILE, TILE)] = scratch[4 * turn + 3][pl.ds(block * count, count), :]
 
 
 def inner_kernel(x_ref, trig_ref, coef_ref, band_ref, rim_ref, sent_ref, ends_ref, y_ref, *scratch):
     del sent_ref, ends_ref
-    row = pl.program_id(0)
+    step = pl.program_id(0)
     _, count, cells = rim_ref.shape
     lines = cells // LANES * 8
-    total_ref = scratch[-1]
-    is_rim = jnp.logical_or(row == 0, row == 7)
-
-    @pl.when(jnp.logical_not(is_rim))
+
+    @pl.when(step < 3)
     def _():
-        local_row(row, x_ref, trig_ref, coef_ref, band_ref, *scratch)
-        for block in range(cells // LANES):
-            value = total_ref[pl.ds(block // 2 * count, count), pl.ds(block % 2 * LANES, LANES)]
-            y_ref[pl.ds(block * 8 + row, count, stride=lines), :] = value
-
-    @pl.when(is_rim)
+        local_pair((2 * step + 1, 2 * step + 2), x_ref, trig_ref, coef_ref, band_ref, *scratch)
+        for turn in range(2):
+            for block in range(cells // LANES):
+                part = pl.ds(block // 2 * count, count)
+                value = scratch[4 * turn + 3][part, pl.ds(block % 2 * LANES, LANES)]
+                y_ref[pl.ds(block * 8 + 2 * step + 1 + turn, count, stride=lines), :] = value
+
+    @pl.when(step == 3)
     def _():
-        for block in range(cells // LANES):
-            value = rim_ref[row // 7, :, pl.ds(block * LANES, LANES)]
-            y_ref[pl.ds(block * 8 + row, count, stride=lines), :] = value
+        for turn in range(2):
+            for block in range(cells // LANES):
+                value = rim_ref[turn, :, pl.ds(block * LANES, LANES)]
+                y_ref[pl.ds(block * 8 + 7 * turn, count, stride=lines), :] = value
 
 
 def expanded(z, table_ref):
@@ -467,11 +486,11 @@
 
     rim = pl.pallas_call(
         rim_kernel,
-        grid=(2,),
+        grid=(1,),
         in_specs=[whole(flat), whole(around), whole(coef), whole(band)],
-        out_specs=pl.BlockSpec((1, circles, cells), lambda i: (i, 0, 0)),
+        out_specs=pl.BlockSpec((2, circles, cells), lambda i: (0, 0, 0)),
         out_shape=jax.ShapeDtypeStruct((2, circles, cells), jnp.float32),
-        scratch_shapes=scratch,
+        scratch_shapes=2 * scratch,
         cost_estimate=cost(2),
         compiler_params=limit,
     )(flat, around, coef, band)
@@ -494,7 +513,7 @@
 
     y = pl.pallas_call(
         inner_kernel,
-        grid=(rows,),
+        grid=(rows // 2,),
         in_specs=[
             whole(flat),
             whole(around),
@@ -506,7 +525,7 @@
         ],
         out_specs=whole(flat),
         out_shape=jax.ShapeDtypeStruct(flat.shape, jnp.float32),
-        scratch_shapes=scratch,
+        scratch_shapes=2 * scratch,
         cost_estimate=cost(rows - 2),
         compiler_params=limit,
     )(flat, around, coef, band, rim, first, rims)

time: 59.5 us -> 57.2 us (0.961)
  Pallas kernels: 43.4 us -> 40.3 us
    pallas_call x2, Pallas kernels: 28.3 us -> 25.2 us  [the longest x1 18.9 us: on_pair(): pl.pallas_call(inner_kernel, grid=(rows // 2,), in_specs=[whole(flat), wh...]
  transfers between devices with their start and end apart: 3 -> 3, of which waited for: 1 -> 1; matrix products, arithmetic and copies ran while one was open for 2% -> 3% of each run, Pallas kernels for 48% -> 44%
where the time goes in v4:
time: 57.2 us; the launch traced here: 56.9 us
  Pallas kernels  40.3 us (70%)
  starting transfers between devices  8.78 us (15%)
  local copies, waits for them, and re-layouts  3.2 us (6%)
  other arithmetic  3.05 us (5%)
  waiting for transfers between devices  1.36 us (2%)
    pallas_call x1, Pallas kernels, on_pair(): pl.pallas_call(inner_kernel, grid=(rows // 2,), in_specs=[whole(flat), wh...  18.9 us
    pallas_call x1, Pallas kernels, on_pair(): pl.pallas_call(final_kernel, grid=(steps,), in_specs=[pl.BlockSpec(memory...  8.54 us
    pallas_call x1, Pallas kernels, on_pair(): pl.pallas_call(rim_kernel, grid=(1,), in_specs=[whole(flat), whole(around...  6.34 us
    pallas_call x1, Pallas kernels, on_pair(): pl.pallas_call(project_kernel, grid=(steps,), in_specs=[four, whole(trig)...  5.68 us
    ppermute x1, starting transfers between devices, on_pair(): lax.ppermute(last, 'lat', [(i, i + 1) for i in range(lat_count - 1)])  4.58 us
    unnamed x18, local copies, waits for them, and re-layouts  2.16 us
    ppermute x1, starting transfers between devices, on_pair(): lax.ppermute(first, 'lat', [(i + 1, i) for i in range(lat_count - 1)])  2.1 us
    ppermute x1, starting transfers between devices, on_pair(): arrived = lax.ppermute(z, 'lon', [(0, 1), (1, 0)])  2.1 us
  transfers between devices with their start and end apart: 3, of which 1 were waited for; matrix products, arithmetic and copies ran while one was open for 3% of the time, Pallas kernels for 44%

profile of v4, /device:TPU:1, one launch (start us, length us, event | category | flops | bytes accessed | tf_op | source)
XLA Modules:
  0.0 56.9 jit_solution(15765781687931091444)
XLA Ops:
  0.0 0.8 %fusion.17 = (f32[1,8,1]{1,2,0:T(1,128)S(1)}, pred[8]{0:T(512)(128)(4,1)S(1)}, s32[8]{0:T(128)S(1)}) fusion(s32[64]{0:T(128)} %param.18, s32[]{:T(128)S(6)} %select_n.41, s32[64]{0:T(128)} %param.17), kind=kLoop, calls=%fused_computation.54 | loop fusion | flops 48 | bytes 140 | tf_op jit(solution)/shard_map/broadcast_in_dim;broadcast_in_dim | solution.py:449
  0.8 0.7 %fusion.15 = (f32[8]{0:T(128)S(1)}, f32[8,1]{0,1:T(1,128)S(1)}, f32[8,1]{0,1:T(1,128)S(1)}) fusion(pred[8]{0:T(512)(128)(4,1)S(1)} %get-tuple-element.10, s32[64]{0:T(128)} %param.17, s32[]{:T(128)S(6)} %select_n.41, s32[8]{0:T(128)S(1)} %get-tuple-element.11), kind=kLoop, calls=%fused_computation.44 | loop fusion | flops 152 | bytes 172 | tf_op jit(solution)/shard_map/mul | solution.py:419
  1.5 0.1 copy.48
  1.6 0.1 copy.53
  1.7 0.1 copy.57.edge_ref
  1.8 0.1 copy.51
  1.9 0.5 fusion.8
  2.3 0.1 multiply_bitcast_fusion.1
  2.4 0.1 slice_multiply_fusion.6
  2.5 0.1 concatenate.13
  2.6 0.1 concatenate.14
  2.7 1.1 %copy-done.1 = bf16[32,8,1536]{2,1,0:T(8,128)(2,1)S(1)} copy-done((bf16[32,8,1536]{2,1,0:T(8,128)(2,1)S(1)}, bf16[32,8,1536]{2,1,0:T(8,128)(2,1)}, u32[]{:S(2)}) %copy-start.1) | copy-done | bytes 786456
  3.8 1.0 %copy-done.4 = bf16[1536,128]{1,0:T(8,128)(2,1)S(1)} copy-done((bf16[1536,128]{1,0:T(8,128)(2,1)S(1)}, bf16[1536,128]{1,0:T(8,128)(2,1)}, u32[]{:S(2)}) %copy-start.4) | copy-done | bytes 393240
  4.8 5.7 %shard_map.110 = f32[3,32,8,128]{3,2,1,0:T(8,128)S(1)} custom-call(f32[3,32,8,1536]{3,2,1,0:T(8,128)} %x_ref.3, f32[2,8,1536]{2,1,0:T(8,128)S(1)} %pad_maximum_fusion.2.trig_ref, f32[2,8,128]{2,1,0:T(8,128)S(1)} %pad_maximum_fusion.4.mix_ref, f32[1,8,1]{2,1,0:T(8,128)S(1)} %copy.57.edge_ref, bf16[32,8,1536]{2,1,0:T(8,128)(2,1)S(1)} %copy-done.1, ...), custom_call_target="tpu_custom_call" | custom-call | tf_op jit(solution)/shard_map/pallas_call | solution.py:460
  10.5 2.1 %collective-permute-start = (f32[3,32,8,128]{3,2,1,0:T(8,128)S(1)}, f32[3,32,8,128]{3,2,1,0:T(8,128)S(1)}, u32[]{:S(2)}, u32[]{:S(2)}) collective-permute-start(f32[3,32,8,128]{3,2,1,0:T(8,128)S(1)} %shard_map.110), channel_id=1, source_target_pairs={{0,1},{1,0},{2,3},{3,2},{4,5},{5,4},{6,7},{7,6},{8,9},{9,8},{10,11... | collective-permute-start | bytes 1179656 | tf_op jit(solution)/shard_map/ppermute | solution.py:468
  12.6 0.5 fusion.12
  13.1 0.1 dynamic-slice_bitcast_fusion.2
  13.3 0.1 copy.46
  13.3 0.1 copy.44
  13.4 0.1 copy.47
  13.5 0.1 copy.45
  13.6 0.1 concatenate.12.coef_ref
  13.7 6.3 %shard_map.109.y_ref.rim_ref = f32[2,96,1536]{2,1,0:T(8,128)S(1)} custom-call(f32[9216,128]{1,0:T(8,128)} %bitcast.41, f32[2,8,3072]{2,1,0:T(8,128)S(1)} %pad_maximum_fusion.trig_ref, f32[8,128]{1,0:T(8,128)S(1)} %concatenate.12.coef_ref, f32[128,3072]{1,0:T(8,128)S(1)} %copy-done.6), custom_call_target="tpu_custom_call" | custom-call | flops 2717908992 | bytes 9437184 | tf_op jit(solution)/shard_map/pallas_call | solution.py:487
  20.1 1.4 %collective-permute-done.z_ref = f32[3,32,8,128]{3,2,1,0:T(8,128)S(1)} collective-permute-done((f32[3,32,8,128]{3,2,1,0:T(8,128)S(1)}, f32[3,32,8,128]{3,2,1,0:T(8,128)S(1)}, u32[]{:S(2)}, u32[]{:S(2)}) %collective-permute-start) | collective-permute-done | bytes 393248 | tf_op jit(solution)/shard_map/ppermute | solution.py:468
  21.4 0.8 %shard_map.111 = (f32[2,32,1536]{2,1,0:T(8,128)S(1)}, f32[2,32,1536]{2,1,0:T(8,128)S(1)}) custom-call(f32[768,128]{1,0:T(8,128)S(1)} %bitcast.40, f32[2,96,1536]{2,1,0:T(8,128)S(1)} %shard_map.109.y_ref.rim_ref, f32[2,8,1536]{2,1,0:T(8,128)S(1)} %pad_maximum_fusion.3.trig_ref, f32[8,128]{1,0:T(8,128)S(1)} %concatenate.12.coef_ref, ...), custom_call_target="tpu_custom_call" | custom-call | tf_op jit(solution)/shard_map/pallas_call | solution.py:500
  22.3 4.6 %collective-permute-start.1 = (f32[2,32,1536]{2,1,0:T(8,128)S(1)}, f32[2,32,1536]{2,1,0:T(8,128)S(1)}, u32[]{:S(2)}, u32[]{:S(2)}) collective-permute-start(f32[2,32,1536]{2,1,0:T(8,128)S(1)} %get-tuple-element.8), channel_id=1, source_target_pairs={{0,2},{2,4},{4,6},{6,8},{8,10},{10,12},{12,14},{1,3},{3,5},{5,7},{... | collective-permute-start | bytes 1179656 | tf_op jit(solution)/shard_map/ppermute | solution.py:508
  26.9 2.1 %collective-permute-start.2 = (f32[2,32,1536]{2,1,0:T(8,128)S(1)}, f32[2,32,1536]{2,1,0:T(8,128)S(1)}, u32[]{:S(2)}, u32[]{:S(2)}) collective-permute-start(f32[2,32,1536]{2,1,0:T(8,128)S(1)} %get-tuple-element.7.sent_ref), channel_id=1, source_target_pairs={{2,0},{4,2},{6,4},{8,6},{10,8},{12,10},{14,12},{3,1},{5,3},{7,5},{... | collective-permute-start | bytes 1179656 | tf_op jit(solution)/shard_map/ppermute | solution.py:509
  29.0 0.2 slice_add_fusion
  29.2 0.1 slice_bitcast_fusion
  29.3 0.1 pad_maximum_fusion.1.ends_ref.rims_ref
  29.4 18.9 %shard_map.112 = f32[9216,128]{1,0:T(8,128)} custom-call(f32[9216,128]{1,0:T(8,128)} %bitcast.42, f32[2,8,3072]{2,1,0:T(8,128)S(1)} %pad_maximum_fusion.trig_ref, f32[8,128]{1,0:T(8,128)S(1)} %concatenate.12.coef_ref, f32[128,3072]{1,0:T(8,128)S(1)} %copy-done.6, f32[2,96,1536]{2,1,0:T(8,128)S(1)} %shard_map.109.y_ref.rim_ref, ...), custom_call_target="tpu_custom_call" | custom-call | flops 8153726976 | bytes 9437184 | tf_op jit(solution)/shard_map/pallas_call | solution.py:514
  48.3 8.5 %shard_map.113 = f32[3,32,8,1536]{3,2,1,0:T(8,128)} custom-call(f32[32]{0:T(128)S(1)} %copy-done.5, f32[3,32,8,1536]{3,2,1,0:T(8,128)} %x_ref.3, f32[3,32,8,1536]{3,2,1,0:T(8,128)} %bitcast.43, f32[3,32,8,128]{3,2,1,0:T(8,128)S(1)} %collective-permute-done.z_ref, f32[2,8,1536]{2,1,0:T(8,128)S(1)} %pad_maximum_fusion.3.trig_ref, ...), custom_call_target="tpu_custom_call" | custom-call | tf_op jit(solution)/shard_map/pallas_call | solution.py:534
  (29 shorter events, 0.2 us)
Async XLA Ops:
  0.0 13.1 %copy-start = (f32[64]{0:T(128)S(1)}, f32[64]{0:T(128)}, u32[]{:S(2)}) copy-start(f32[64]{0:T(128)} %param.13) | copy-start | bytes 772
  0.0 13.2 %copy-start.7 = (f32[64]{0:T(128)S(1)}, f32[64]{0:T(128)}, u32[]{:S(2)}) copy-start(f32[64]{0:T(128)} %param.15) | copy-start | bytes 772
  0.0 13.2 %copy-start.8 = (f32[64]{0:T(128)S(1)}, f32[64]{0:T(128)}, u32[]{:S(2)}) copy-start(f32[64]{0:T(128)} %param.14) | copy-start | bytes 772
  2.7 1.1 %copy-start.1 = (bf16[32,8,1536]{2,1,0:T(8,128)(2,1)S(1)}, bf16[32,8,1536]{2,1,0:T(8,128)(2,1)}, u32[]{:S(2)}) copy-start(bf16[32,8,1536]{2,1,0:T(8,128)(2,1)} %depth_ref.5) | copy-start | bytes 2359300
  3.8 1.0 %copy-start.4 = (bf16[1536,128]{1,0:T(8,128)(2,1)S(1)}, bf16[1536,128]{1,0:T(8,128)(2,1)}, u32[]{:S(2)}) copy-start(bf16[1536,128]{1,0:T(8,128)(2,1)} %constant.64.clone.table_ref) | copy-start | bytes 1179652
  4.8 8.9 %copy-start.6 = (f32[128,3072]{1,0:T(8,128)S(1)}, f32[128,3072]{1,0:T(8,128)}, u32[]{:S(2)}) copy-start(f32[128,3072]{1,0:T(8,128)} %constant.66.clone.band_ref) | copy-start | bytes 4718596
  10.5 10.9 %collective-permute-start = (f32[3,32,8,128]{3,2,1,0:T(8,128)S(1)}, f32[3,32,8,128]{3,2,1,0:T(8,128)S(1)}, u32[]{:S(2)}, u32[]{:S(2)}) collective-permute-start(f32[3,32,8,128]{3,2,1,0:T(8,128)S(1)} %shard_map.110), channel_id=1, source_target_pairs={{0,1},{1,0},{2,3},{3,2},{4,5},{5,4},{6,7},{7,6},{8,9},{9,8},{10,11... | collective-permute-start | bytes 1179656 | tf_op jit(solution)/shard_map/ppermute | solution.py:468
  13.7 7.7 %copy-start.2 = (bf16[32,8,1536]{2,1,0:T(8,128)(2,1)S(1)}, bf16[32,8,1536]{2,1,0:T(8,128)(2,1)}, u32[]{:S(2)}) copy-start(bf16[32,8,1536]{2,1,0:T(8,128)(2,1)} %depth_ref.5) | copy-start | bytes 2359300
  13.7 7.7 %copy-start.3 = (bf16[256,1536]{1,0:T(8,128)(2,1)S(1)}, bf16[256,1536]{1,0:T(8,128)(2,1)}, u32[]{:S(2)}) copy-start(bf16[256,1536]{1,0:T(8,128)(2,1)} %constant.65.clone.expand_ref) | copy-start | bytes 2359300
  22.3 26.0 %collective-permute-start.1 = (f32[2,32,1536]{2,1,0:T(8,128)S(1)}, f32[2,32,1536]{2,1,0:T(8,128)S(1)}, u32[]{:S(2)}, u32[]{:S(2)}) collective-permute-start(f32[2,32,1536]{2,1,0:T(8,128)S(1)} %get-tuple-element.8), channel_id=1, source_target_pairs={{0,2},{2,4},{4,6},{6,8},{8,10},{10,12},{12,14},{1,3},{3,5},{5,7},{... | collective-permute-start | bytes 1179656 | tf_op jit(solution)/shard_map/ppermute | solution.py:508
  26.9 21.5 %collective-permute-start.2 = (f32[2,32,1536]{2,1,0:T(8,128)S(1)}, f32[2,32,1536]{2,1,0:T(8,128)S(1)}, u32[]{:S(2)}, u32[]{:S(2)}) collective-permute-start(f32[2,32,1536]{2,1,0:T(8,128)S(1)} %get-tuple-element.7.sent_ref), channel_id=1, source_target_pairs={{2,0},{4,2},{6,4},{8,6},{10,8},{12,10},{14,12},{3,1},{5,3},{7,5},{... | collective-permute-start | bytes 1179656 | tf_op jit(solution)/shard_map/ppermute | solution.py:509
  29.4 18.9 %copy-start.5 = (f32[32]{0:T(128)S(1)}, f32[32]{0:T(128)}, u32[]{:S(2)}) copy-start(f32[32]{0:T(128)} %weight_ref.1) | copy-start | bytes 388
